TPU v7x, 256 devices: a whole 4x4x8 slice. The times are simulated.
256 devices in a mesh: dp: 4 (over z_hi), shard: 64 (over y, z_lo, x, core).
Axes of the slice: x: 4, y: 4, z: 8 (z_hi: 4, z_lo: 2; z = z_hi * 2 + z_lo), core: 2. Of those that a mesh axis runs over, the one named last changes fastest.
Arguments:
- block_input: bfloat16 [512, 14, 14, 1584], P(('dp', 'shard')), may hold values from -16 to 16
- upstream: bfloat16 [512, 14, 14, 1584], P(('dp', 'shard')), may hold values from -8 to 8
- kernel_tiles: bfloat16 [256, 13068], P('shard'), may hold values from -0.1875 to 0.1875
- tile_counts: int32 [64], replicated, may hold values from 1 to 4, 144 in all
- owner_order: int32 [64], replicated, may hold values from 0 to 63, each once
- gain: float32 [1584], replicated, may hold values from 0.5 to 1.5
- bias: float32 [1584], replicated, may hold values from -2.5 to 2.5
Outputs:
- block_out: bfloat16 [512, 14, 14, 1584], P(('dp', 'shard'))
- input_grad: bfloat16 [512, 14, 14, 1584], P(('dp', 'shard'))
- kernel_grad: float32 [1881792], P('shard')
- gain_grad: float32 [1584], replicated
- bias_grad: float32 [1584], replicated
Inputs may be any that keep to these rules, and one draw needn't show every extreme that they name: `tile_counts`: entry k is the number of kernel tiles held by the k-th rank of the owner order; the entries sum to 144. `owner_order`: every shard index appears once.
All inputs are finite; a program needn't handle non-finite values.
Results may differ from a plain program's by a relative error of at most 0.019.
Values may be sent and summed in bfloat16 or wider, within the bound.
A program may use at most 192 MiB of HBM per device.

v0:
```python
import jax
import jax.numpy as jnp
from jax import lax
from jax.sharding import PartitionSpec as P

GW = 132
HH = 14
WW = 14
GROUPS = 12
KSIZE = 1881792


EPSILON = 1e-05


def tile_rows(tile_counts, owner_order, capacity, total_tiles):
    ranks_total = tile_counts.shape[0]
    run_start = jnp.cumsum(tile_counts) - tile_counts
    run_end = run_start + tile_counts
    tile_ids = jnp.arange(total_tiles, dtype=jnp.int32)
    rank_of = jnp.sum((run_end[None, :] <= tile_ids[:, None]).astype(jnp.int32), axis=1)
    onehot = (rank_of[:, None] == jnp.arange(ranks_total, dtype=jnp.int32)[None, :]).astype(
        jnp.int32
    )
    holder = jnp.sum(onehot * owner_order[None, :], axis=1)
    begins = jnp.sum(onehot * run_start[None, :], axis=1)
    return holder * capacity + tile_ids - begins


def silu_slope(values):
    sigma = jax.nn.sigmoid(values)
    return sigma * (1.0 + values * (1.0 - sigma))


def tap_columns(maps, groups, mirrored):
    number, height, breadth, channels = maps.shape
    group_width = channels // groups
    padded = jnp.pad(maps, ((0, 0), (1, 1), (1, 1), (0, 0)))
    pieces = []
    for position in range(9):
        row_off, col_off = (position // 3, position % 3)
        if mirrored:
            row_off, col_off = (2 - row_off, 2 - col_off)
        window = padded[:, row_off : row_off + height, col_off : col_off + breadth, :]
        pieces.append(window.reshape(number * height * breadth, groups, group_width))
    return jnp.stack(pieces, axis=2)


def local(block_input, upstream, kernel_tiles, tile_counts, owner_order, gain, bias):
    capacity = kernel_tiles.shape[0]
    tile_len = kernel_tiles.shape[1]
    gathered = lax.all_gather(kernel_tiles, "shard", axis=0, tiled=True)
    row_index = tile_rows(tile_counts, owner_order, capacity, KSIZE // tile_len)
    kernel = gathered[row_index].reshape(GROUPS, 9, GW, GW)
    number, height, breadth, channels = block_input.shape
    input_columns = tap_columns(block_input, GROUPS, False)
    hidden = jnp.einsum("rgti,gtio->rgo", input_columns, kernel, preferred_element_type=jnp.float32)
    hidden = hidden.reshape(number, height, breadth, channels).astype(jnp.bfloat16)
    values = lax.optimization_barrier(hidden).astype(jnp.float32)
    row_total = number * HH * WW * lax.axis_size("dp") * lax.axis_size("shard")
    moment_one, moment_two = lax.psum(
        (jnp.sum(values, axis=(0, 1, 2)), jnp.sum(values * values, axis=(0, 1, 2))), ("dp", "shard")
    )
    average = moment_one / row_total
    inv_std = lax.rsqrt(moment_two / row_total - average * average + EPSILON)
    normed = (values - average) * inv_std
    affine = gain * normed + bias
    summed = block_input.astype(jnp.float32) + jax.nn.silu(affine)
    block_out = jax.nn.silu(summed).astype(jnp.bfloat16)
    grad_sum = upstream.astype(jnp.float32) * silu_slope(summed)
    grad_affine = grad_sum * silu_slope(affine)
    gain_grad, bias_grad = lax.psum(
        (jnp.sum(grad_affine * normed, axis=(0, 1, 2)), jnp.sum(grad_affine, axis=(0, 1, 2))),
        ("dp", "shard"),
    )
    grad_hidden = (
        gain * inv_std * (grad_affine - bias_grad / row_total - normed * gain_grad / row_total)
    ).astype(jnp.bfloat16)
    grad_columns = tap_columns(grad_hidden, GROUPS, True)
    backward = jnp.einsum(
        "rgto,gtio->rgi", grad_columns, kernel, preferred_element_type=jnp.float32
    )
    input_grad = (grad_sum + backward.reshape(number, height, breadth, channels)).astype(
        jnp.bfloat16
    )
    grad_rows = grad_hidden.reshape(number * height * breadth, GROUPS, channels // GROUPS)
    local_term = jnp.einsum(
        "rgti,rgo->gtio", input_columns, grad_rows, preferred_element_type=jnp.float32
    ).astype(jnp.bfloat16)
    widened = lax.optimization_barrier(local_term).astype(jnp.float32).reshape(-1)
    shard_piece = lax.psum_scatter(widened, "shard", scatter_dimension=0, tiled=True)
    kernel_grad = lax.psum(shard_piece.astype(jnp.bfloat16), "dp").astype(jnp.float32)
    return (block_out, input_grad, kernel_grad, gain_grad, bias_grad)


def solution(mesh):
    return jax.shard_map(
        local,
        mesh=mesh,
        in_specs=(
            P(("dp", "shard"), None, None, None),
            P(("dp", "shard"), None, None, None),
            P("shard", None),
            P(),
            P(),
            P(),
            P(),
        ),
        out_specs=(
            P(("dp", "shard"), None, None, None),
            P(("dp", "shard"), None, None, None),
            P("shard"),
            P(),
            P(),
        ),
        check_vma=False,
    )
```

profile of v0, /device:TPU:1, one launch (start us, length us, event | category | flops | bytes accessed | tf_op | source)
XLA Modules:
  0.0 961.1 jit_solution(17396444134386787720)
XLA Ops:
  9.4 10.9 %pad_slice_fusion.8 = (bf16[2,14,14,1584]{3,0,2,1:T(2,128)(2,1)}, bf16[2,14,14,1584]{3,0,2,1:T(2,128)(2,1)}, bf16[2,14,14,1584]{3,0,2,1:T(2,128)(2,1)}, bf16[2,1...) fusion(bf16[2,14,14,1584]{3,0,2,1:T(2,128)(2,1)S(1)} %copy-done), kind=kLoop, calls=%fused_computation.73 | loop fusion | bytes 11176704 | tf_op jit(solution)/shard_map/slice | solution.py:44
  21.6 8.5 stack_reshape.54
  30.1 5.8 copy.117
  35.9 2.6 copy.109
  38.5 8.5 stack_reshape.55
  47.0 5.8 copy.118
  52.8 2.6 copy.110
  55.4 8.5 stack_reshape.56
  63.9 5.7 copy.119
  69.6 2.6 copy.111
  72.2 8.5 stack_reshape.57
  80.7 5.8 copy.120
  86.5 7.9 stack_reshape.58
  94.4 5.8 copy.121
  101.6 8.1 stack_reshape.59
  109.8 5.8 copy.122
  117.0 7.9 stack_reshape.60
  125.0 5.7 copy.123
  132.2 7.9 stack_reshape.61
  140.1 5.8 copy.124
  147.3 7.9 stack_reshape.62
  155.3 5.8 copy.125
  162.9 2.9 constant_dynamic-update-slice_fusion.8
  165.7 2.9 constant_dynamic-update-slice_fusion.7
  178.0 11.2 %reshape.110 = bf16[256,13068]{1,0:T(8,128)(2,1)} reshape(bf16[64,4,13068]{2,1,0:T(4,128)(2,1)} %all-gather.3.cloned.1.call-done) | data formatting | bytes 13381632
  189.2 12.0 %gather_fusion = bf16[144,13068]{1,0:T(8,128)(2,1)} fusion(bf16[256,13068]{1,0:T(8,128)(2,1)} %reshape.110, s32[1024]{0:T(1024)S(1)} %pad_clamp_fusion), kind=kCustom, calls=%fused_computation | custom fusion | bytes 7527744 | tf_op jit(solution)/shard_map/gather | solution.py:54
  201.2 13.3 %reshape.94 = bf16[12,9,132,132]{3,2,1,0:T(8,128)(2,1)} reshape(bf16[144,13068]{1,0:T(8,128)(2,1)} %gather_fusion) | data formatting | bytes 7527168 | tf_op jit(solution)/shard_map/reshape | solution.py:54
  214.5 11.4 %fusion.22 = bf16[392,12,132]{0,2,1:T(8,128)(2,1)} fusion(bf16[12,9,132,132]{3,2,1,0:T(8,128)(2,1)} %reshape.94, bf16[392,12,9,132]{0,3,2,1:T(8,128)(2,1)} %constant_dynamic-update-slice_fusion), kind=kOutput, calls=%fused_computation.33 | convolution fusion | flops 1475945856 | bytes 16182144 | tf_op jit(solution)/shard_map/rgti,gtio->rgo/dot_general | solution.py:57
  225.9 7.2 copy.127
  233.1 5.6 convert_element_type.48
  239.2 81.6 %all-reduce.4 = (f32[1584]{0:T(1024)S(1)}, f32[1584]{0:T(1024)S(1)}) all-reduce(f32[1584]{0:T(1024)S(1)} %get-tuple-element.23, f32[1584]{0:T(1024)S(1)} %get-tuple-element.22), channel_id=1, replica_groups=mesh['dp'=4,'shard'=64] {'dp','shard'}, use_global_device_ids=true, to_apply=%region_7.8 | all-reduce | flops 3168 | bytes 25344 | tf_op jit(solution)/shard_map/psum | solution.py:61
  320.8 5.3 fusion.24
  326.1 72.7 %all-reduce.3 = (f32[1584]{0:T(1024)S(1)}, f32[1584]{0:T(1024)S(1)}) all-reduce(f32[1584]{0:T(1024)S(1)} %get-tuple-element.21, f32[1584]{0:T(1024)S(1)} %get-tuple-element.20), channel_id=1, replica_groups=mesh['dp'=4,'shard'=64] {'dp','shard'}, use_global_device_ids=true, to_apply=%region_11.12 | all-reduce | flops 3168 | bytes 25344 | tf_op jit(solution)/shard_map/psum | solution.py:72
  398.9 2.7 fusion.19
  401.6 7.9 reshape.96
  409.5 5.2 pad_slice_fusion
  414.7 8.0 stack_reshape.67
  422.6 13.3 %convolution_convert_fusion = bf16[12,9,132,132]{3,2,1,0:T(8,128)(2,1)} fusion(bf16[392,12,9,132]{0,3,2,1:T(8,128)(2,1)} %constant_dynamic-update-slice_fusion, bf16[392,12,132,1]{2,1,0,3:T(8,128)(2,1)} %bitcast.26), kind=kOutput, calls=%fused_computation.1 | convolution fusion | flops 1477206784 | bytes 16182144 | tf_op jit(solution)/shard_map/rgti,rgo->gtio/dot_general | solution.py:87
  436.0 18.4 %reshape.100 = f32[1881792]{0:T(1024)} reshape(bf16[12,9,132,132]{3,2,1,0:T(8,128)(2,1)} %convolution_convert_fusion) | data formatting | bytes 11290752 | tf_op jit(solution)/shard_map/reshape | solution.py:90
  454.4 318.2 %all-reduce.6 = bf16[1881792]{0:T(1024)(128)(2,1)} all-reduce(f32[1881792]{0:T(1024)} %reshape.100), channel_id=2, replica_groups=mesh['dp'=4,'shard'=64] {'shard'}, use_global_device_ids=true, to_apply=%region_12.13.clone | all-reduce | flops 1881792 | bytes 11290752
  773.5 14.6 %psum.39 = bf16[29403]{0:T(1024)(128)(2,1)S(1)} all-reduce(bf16[29403]{0:T(1024)(128)(2,1)S(1)} %dynamic-slice.3), channel_id=1, replica_groups=mesh['dp'=4,'shard'=64] {'dp'}, use_global_device_ids=true, to_apply=%region_13.14 | all-reduce | flops 29403 | bytes 117612 | tf_op jit(solution)/shard_map/psum | solution.py:92
  788.8 8.0 stack_reshape.63
  796.8 5.0 copy.129
  803.1 8.6 stack_reshape.64
  811.7 5.0 copy.130
  816.7 8.6 stack_reshape.65
  825.2 5.7 copy.131
  831.0 8.6 stack_reshape.66
  839.5 5.8 copy.132
  845.3 5.8 copy.133
  851.1 8.6 stack_reshape.68
  859.6 5.8 copy.134
  865.4 8.6 stack_reshape.69
  873.9 6.0 copy.135
  879.9 8.6 stack_reshape.70
  888.5 5.7 copy.136
  894.2 8.6 stack_reshape.71
  902.8 5.8 copy.137
  920.6 10.0 %convolution_bitcast_fusion = f32[392,12,132]{0,2,1:T(8,128)} fusion(bf16[12,9,132,132]{3,2,1,0:T(8,128)(2,1)S(1)} %bitcast.25, bf16[392,12,9,132]{0,3,2,1:T(8,128)(2,1)} %constant_dynamic-update-slice_fusion.9), kind=kOutput, calls=%fused_computation.32 | convolution fusion | flops 1475324928 | bytes 17424000 | tf_op jit(solution)/shard_map/rgto,gtio->rgi/dot_general | solution.py:80
  930.6 8.1 copy.138
  938.8 7.1 reshape.95
  945.8 4.0 add_convert_fusion
  949.8 2.1 copy.140
  951.9 2.1 copy.141
  (93 shorter events, 35.4 us)
Async XLA Ops:
  7.2 2.2 copy-start
  7.2 170.8 %all-gather.3.cloned.1.call-start = ((), (), s32[]{:S(2)}) async-start(), calls=%async_computation | async-start | bytes 6855680 | tf_op jit(solution)/shard_map/all_gather | solution.py:52
  155.3 5.8 copy-start.21
  155.3 6.1 copy-start.23
  155.3 7.4 copy-start.22
  162.8 5.7 copy-start.2
  165.7 4.2 copy-start.3
  168.6 2.7 copy-start.4
  170.0 2.7 copy-start.5
  171.3 2.6 copy-start.6
  172.7 2.7 copy-start.7
  174.0 2.7 copy-start.8
  233.1 87.7 %copy-start.17 = (f32[1584]{0:T(1024)S(1)}, f32[1584]{0:T(1024)}, u32[]{:S(2)}) copy-start(f32[1584]{0:T(1024)} %param.12) | copy-start | bytes 19012
  233.1 87.7 %copy-start.18 = (f32[1584]{0:T(1024)S(1)}, f32[1584]{0:T(1024)}, u32[]{:S(2)}) copy-start(f32[1584]{0:T(1024)} %param.13) | copy-start | bytes 19012
  398.9 2.7 copy-start.19
  398.9 2.7 copy-start.20
  454.4 334.4 %copy-start.16 = (bf16[2,14,14,1584]{3,2,1,0:T(8,128)(2,1)S(1)}, bf16[2,14,14,1584]{3,2,1,0:T(8,128)(2,1)}, u32[]{:S(2)}) copy-start(bf16[2,14,14,1584]{3,2,1,0:T(8,128)(2,1)} %get-tuple-element.40) | copy-start | bytes 3725572
  908.5 2.0 copy-start.9
  908.5 3.4 copy-start.11
  910.6 2.7 copy-start.10
  912.0 2.7 copy-start.12
  913.3 2.6 copy-start.13
  913.3 7.3 slice-start
  914.6 3.4 copy-start.14
  915.9 3.4 copy-start.15
  915.9 4.7 slice-start.1
  938.7 7.1 copy-start.1
Sparse Core Ops, SparseCore 0:
  9.9 116.2 all-gather.2
where the time goes:
time: 980 us; the launch traced here: 961 us
  blocking collectives  487 us (50%)
  local copies, waits for them, and re-layouts  410 us (42%)
  matrix products  34.7 us (4%)
  between operations  15.3 us (2%)
  other arithmetic  13.6 us (1%)
    unnamed x1, blocking collectives  318 us
    another operation x38, local copies, waits for them, and re-layouts, tap_columns(): return jnp.stack(pieces, axis=2)  255 us
    psum x1, blocking collectives, local(): lax.psum((jnp.sum(values, axis=(0, 1, 2)), jnp.sum(values * values, axis=...  81.6 us
    psum x1, blocking collectives, local(): lax.psum((jnp.sum(grad_affine * normed, axis=(0, 1, 2)), jnp.sum(grad_aff...  72.7 us
    unnamed x74, local copies, waits for them, and re-layouts  44.3 us
    slice x10, local copies, waits for them, and re-layouts, tap_columns(): window = padded[:, row_off:row_off + height, col_off:col_off + breadth, :]  31.1 us
  transfers between devices with their start and end apart: 1, of which 0 were waited for; matrix products, arithmetic and copies ran while one was open for 18% of the time, Pallas kernels for 0%

commit v1 on v0

v1 whole, which is shorter than its diff:
```python
import numpy as np
import jax
import jax.numpy as jnp
from jax import lax
from jax.experimental import pallas as pl
from jax.experimental.pallas import tpu as pltpu
from jax.sharding import PartitionSpec as P

GROUPS = 12
GW = 132
ROWS = 448
LANES = 1664
BF = jnp.bfloat16
F32 = jnp.float32
EPSILON = 1e-05
TOTAL = 100352
VLIM = 60 * 1024 * 1024


def extra_lane(g, a):
    return 16 * (g // 3) + 4 * (g % 3) + a


def constants():
    pg = np.zeros((GROUPS, 256, 256), np.float32)
    for g in range(GROUPS):
        for j in range(GW):
            a, l = j // 33, j % 33
            pg[g, 4 * g + j, 32 * a + l if l < 32 else 128 + extra_lane(g, a)] = 1
    ry = np.zeros((9, 128, 4, 128), np.float32)
    for g in range(GROUPS):
        for tap in range(9):
            for a in range(4):
                ry[tap, extra_lane(g, a), g // 3, 36 * (g % 3) + 4 * tap + a] = 1
    selm = np.zeros((GROUPS, 16, 128), np.float32)
    for g in range(GROUPS):
        for a in range(4):
            selm[g, 3 + a, extra_lane(g, a)] = 1
    sele = np.zeros((2, 3, 128, 12, 16), np.float32)
    selb = np.zeros((2, 3, 9, 16, 12, 16), np.float32)
    for gg in range(3):
        for u in range(36):
            q, j = u // 3, u % 3
            tap, a = u // 4, u % 4
            for kind, row in ((0, j), (1, 7 + j)):
                sele[kind, gg, 36 * gg + u, q, row] = 1
                selb[kind, gg, tap, 4 * gg + a, q, row] = 1
    bf = lambda v, *s: jnp.asarray(v.reshape(s), BF)
    return dict(
        pg=bf(pg, GROUPS, 256, 256),
        ry=bf(ry, 1152, 512),
        selm=bf(selm, 192, 128),
        sele=bf(sele, 2, 3, 128, 192),
        selb=bf(selb, 2, 3, 144, 192),
    )


def prep_constants():
    cs = np.zeros((GW, 128), np.float32)
    cse = np.zeros((GW, 112), np.float32)
    csee = np.zeros((GW, 128), np.float32)
    rs = np.zeros((112, 99), np.float32)
    rsm = np.zeros((99, 128), np.float32)
    rse = np.zeros((112, 99), np.float32)
    for a in range(4):
        for l in range(32):
            cs[33 * a + l, 32 * a + l] = 1
        cse[33 * a + 32, 99 + a] = 1
    for lane in range(128):
        csee[33 * (lane % 4) + 32, lane] = 1
    for j in range(3):
        for l in range(32):
            rs[32 * j + l, 33 * j + l] = 1
            rsm[33 * j + l, 32 * j + l] = 1
        rs[96 + j, 33 * j + 32] = 1
        rse[103 + j, 33 * j + 32] = 1
    return [jnp.asarray(v, BF) for v in (cs, cse, csee, rs, rsm, rse)]


def dot(a, b, dims=((1,), (0,))):
    return lax.dot_general(a, b, (dims, ((), ())), preferred_element_type=F32)


def prep_body(tile_ref, cs, cse, csee, rs, rsm, rse, out_ref):
    for s in range(4):
        t = tile_ref[s]
        u = dot(t, cs[...]).astype(BF)
        ue = dot(t, cse[...]).astype(BF)
        uee = dot(t, csee[...]).astype(BF)
        v = dot(rs[...], u) + dot(ue, rsm[...], ((0,), (0,))) + dot(rse[...], uee)
        out_ref[s] = v.astype(BF)


def prep(tiles):
    return pl.pallas_call(
        prep_body,
        out_shape=jax.ShapeDtypeStruct((4, 112, 128), BF),
        name="prep",
    )(tiles, *prep_constants())


def lanes_of(g, width=1):
    return pl.ds(pl.multiple_of(g * 128, 128), 128 * width)


def lane_iota(rows):
    return lax.broadcasted_iota(jnp.int32, (rows, 128), 1)


def load_native(src, xn):
    xn[...] = jnp.zeros_like(xn)
    for n in range(2):
        for y in range(14):
            xn[n * 14 + y, 0:14, 0:1584] = src[n, y]


def store_shifts(dst, main, lanes):
    for b in range(3):
        moved = main if b == 1 else pltpu.roll(main, (1 - b) % ROWS, 0)
        dst[b, :, 1:15, :, lanes] = moved.astype(BF).reshape(2, 14, 16, 128)


def zero_borders(dst):
    zeros = jnp.zeros((3, 2, 16, LANES), BF)
    dst[:, :, 0] = zeros
    dst[:, :, 15] = zeros


def tap_slice(src, tap, lanes, mirrored):
    a, b = tap // 3, tap % 3
    if mirrored:
        a, b = 2 - a, 2 - b
    return src[b, :, a : a + 14, :, lanes].reshape(ROWS, 128)


def tap_concat(src, lanes, mirrored, extra=None):
    pieces = [tap_slice(src, tap, lanes, mirrored) for tap in range(9)]
    if extra is not None:
        pieces.append(extra)
    return jnp.concatenate(pieces, axis=1)


def permute_in(xn, pg, sink, acc):
    acc[...] = jnp.zeros_like(acc)

    def step(g, carry):
        r = dot(xn[:, :, lanes_of(g, 2)].reshape(ROWS, 256), pg[g])
        sink(g, r[:, :128])
        acc[...] += r[:, 128:]
        return carry

    lax.fori_loop(0, GROUPS, step, 0)
    sink(GROUPS, acc[...])


def permute_out(src, pg, out_ref, on):
    def step(g, carry):
        pair = jnp.concatenate([src(g), src(GROUPS)], axis=1)
        r = dot(pair, pg[g], ((1,), (1,)))
        on[:, :, lanes_of(g)] = (carry + r[:, :128]).astype(BF).reshape(28, 16, 128)
        return r[:, 128:]

    carry = lax.fori_loop(0, GROUPS, step, jnp.zeros((ROWS, 128), F32))
    on[:, :, 1536:1664] = carry.astype(BF).reshape(28, 16, 128)
    for n in range(2):
        for y in range(14):
            out_ref[n, y] = on[n * 14 + y, 0:14, 0:1584]


def fwd_body(idx, x_ref, g_ref, pg, ry, selm, sele, xb, ex, hid, bm, ta, me, sums, xn, acc, bg):
    load_native(x_ref, xn)
    zero_borders(xb)
    permute_in(xn, pg, lambda g, v: store_shifts(xb, v, lanes_of(g)), acc)
    ex[...] = dot(tap_concat(xb, pl.ds(1536, 128), False), ry[...]).astype(BF)

    def pull(t, carry):
        g, q = t // 12, t % 12
        s = idx[t]
        bm[g, pl.ds(pl.multiple_of(q * 96, 32), 96), :] = g_ref[s, 0:96, :]
        ta[g, q] = g_ref[s, 96:112, :]
        return carry

    lax.fori_loop(0, 144, pull, 0)
    for q in range(12):
        m = dot(ta[:, q].reshape(192, 128), selm[...], ((0,), (0,)))
        me[96 * q : 96 * q + 96, :] = m[0:96].astype(BF)

    acc[...] = jnp.zeros_like(acc)
    valid = (lax.broadcasted_iota(jnp.int32, (ROWS, 128), 0) % 16) < 14

    def stat(h, lanes):
        h = jnp.where(valid, h.astype(F32), 0.0)
        sums[0:1, lanes] = jnp.sum(h, axis=0, keepdims=True)
        sums[1:2, lanes] = jnp.sum(h * h, axis=0, keepdims=True)

    def step(g, carry):
        gg = g % 3
        mine = (lane_iota(1152) // 4) == (g // 3) * 4 + gg
        bg[0:1152, 0:128] = bm[g]
        bg[0:1152, 128:256] = jnp.where(mine, me[...].astype(F32), 0.0).astype(BF)
        tails = ta[g].reshape(192, 128)
        bg[1152:1280, 0:128] = dot(sele[0, gg], tails).astype(BF)
        ee = jnp.where(mine[0:128], dot(sele[1, gg], tails), 0.0)
        bg[1152:1280, 128:256] = ee.astype(BF)
        a = tap_concat(xb, lanes_of(g), False, ex[:, lanes_of(g // 3)])
        r = dot(a, bg[...])
        h = r[:, :128].astype(BF)
        hid[:, lanes_of(g)] = h
        stat(h, lanes_of(g))
        acc[...] += r[:, 128:]
        return carry

    lax.fori_loop(0, GROUPS, step, 0)
    h = acc[...].astype(BF)
    hid[:, 1536:1664] = h
    stat(h, pl.ds(1536, 128))


SM = pltpu.SMEM
VM = pltpu.VMEM


def vspec():
    return pl.BlockSpec(memory_space=VM)


def sspec():
    return pl.BlockSpec(memory_space=SM)


def struct(shape, dtype):
    return jax.ShapeDtypeStruct(shape, dtype)


def fwd(idx, x, gathered, c):
    return pl.pallas_call(
        fwd_body,
        in_specs=[sspec()] + [vspec()] * 6,
        out_specs=[vspec()] * 7,
        out_shape=[
            struct((3, 2, 16, 16, LANES), BF),
            struct((ROWS, 512), BF),
            struct((ROWS, LANES), BF),
            struct((GROUPS, 1152, 128), BF),
            struct((GROUPS, 12, 16, 128), BF),
            struct((1152, 128), BF),
            struct((2, LANES), F32),
        ],
        scratch_shapes=[
            VM((28, 16, LANES), BF),
            VM((ROWS, 128), F32),
            VM((1280, 256), BF),
        ],
        compiler_params=pltpu.CompilerParams(vmem_limit_bytes=VLIM),
        name="fwd",
    )(idx, x, gathered, c["pg"], c["ry"], c["selm"], c["sele"])


def half_tanh(v):
    return 0.5 * jnp.tanh(0.5 * v) + 0.5


def norm_body(up_ref, xb, hid, sums, par, pg, out_ref, gs, ga, gsum, xn, on, upp, bo, acc):
    load_native(up_ref, xn)

    def keep(g, v):
        upp[:, lanes_of(g)] = v.astype(BF)

    permute_in(xn, pg, keep, acc)

    def tile(t, carry):
        lanes = lanes_of(t)
        avg = sums[0:1, lanes] / TOTAL
        inv = lax.rsqrt(sums[1:2, lanes] / TOTAL - avg * avg + EPSILON)
        gain, bias = par[0:1, lanes], par[1:2, lanes]
        s1 = jnp.zeros((8, 128), F32)
        s2 = jnp.zeros((8, 128), F32)
        for k in range(28):
            rows = pl.ds(16 * k, 16)
            n, y = k // 14, k % 14
            x = xb[1, n, y + 1, :, lanes].astype(F32)
            normed = (hid[rows, lanes].astype(F32) - avg) * inv
            aff = gain * normed + bias
            sa = half_tanh(aff)
            act = aff * sa
            summed = x + act
            ss = half_tanh(summed)
            out = summed * ss
            bo[rows, lanes] = out.astype(BF)
            gsv = upp[rows, lanes].astype(F32) * (ss + out * (1.0 - ss))
            gav = gsv * (sa + act * (1.0 - sa))
            gs[rows, lanes] = gsv
            ga[rows, lanes] = gav
            p = gav * normed
            s1 = s1 + (p[0:8] + p[8:16])
            s2 = s2 + (gav[0:8] + gav[8:16])
        gsum[0:1, lanes] = jnp.sum(s1, axis=0, keepdims=True)
        gsum[1:2, lanes] = jnp.sum(s2, axis=0, keepdims=True)
        return carry

    lax.fori_loop(0, 13, tile, 0)
    permute_out(lambda g: bo[:, lanes_of(g)], pg, out_ref, on)


def norm(up, xb, hid, sums, par, c):
    return pl.pallas_call(
        norm_body,
        in_specs=[vspec()] * 6,
        out_specs=[vspec()] * 4,
        out_shape=[
            struct((2, 14, 14, 1584), BF),
            struct((ROWS, LANES), F32),
            struct((ROWS, LANES), F32),
            struct((2, LANES), F32),
        ],
        scratch_shapes=[
            VM((28, 16, LANES), BF),
            VM((28, 16, LANES), BF),
            VM((ROWS, LANES), BF),
            VM((ROWS, LANES), BF),
            VM((ROWS, 128), F32),
        ],
        compiler_params=pltpu.CompilerParams(vmem_limit_bytes=VLIM),
        name="norm",
    )(up, xb, hid, sums, par, c["pg"])


def piece_of(b):
    one = lambda cond: jnp.where(cond, 1, 0)
    late = b >= 13
    xa = one(b >= 3) + one(b >= 7) + one(b >= 10)
    xl = one(b >= 17) + one(b >= 20) + one(b >= 24)
    sa = 3 * one(b >= 3) + 4 * one(b >= 7) + 3 * one(b >= 10)
    sl = 13 + 4 * one(b >= 17) + 3 * one(b >= 20) + 4 * one(b >= 24)
    first = jnp.where(xl == 1, 4, 3)
    x = jnp.where(late, xl, xa)
    pos = jnp.where(late, b - sl + first, b - sa)
    return x, pos


def back_body(hid, sums, gsum, par, gs, ga, xb, ex, bm, ta, me, pg, ry, selb, ig_ref, st,
              ghb, eg, tr, wt, tot, acc, on, mec):
    zero_borders(ghb)
    valid = (lax.broadcasted_iota(jnp.int32, (ROWS, 128), 0) % 16) < 14

    def tile(t, carry):
        lanes = lanes_of(t)
        avg = sums[0:1, lanes] / TOTAL
        inv = lax.rsqrt(sums[1:2, lanes] / TOTAL - avg * avg + EPSILON)
        scale = par[0:1, lanes] * inv
        c1 = gsum[1:2, lanes] / TOTAL
        c2 = gsum[0:1, lanes] / TOTAL
        normed = (hid[:, lanes].astype(F32) - avg) * inv
        gh = scale * (ga[:, lanes] - c1 - normed * c2)
        gh = jnp.where(valid, gh, 0.0)
        store_shifts(ghb, gh, lanes)
        return carry

    lax.fori_loop(0, 13, tile, 0)
    eg[...] = dot(tap_concat(ghb, pl.ds(1536, 128), True), ry[...]).astype(BF)
    g12 = ghb[1, :, 1:15, :, pl.ds(1536, 128)].reshape(ROWS, 128)
    g12t = g12.astype(F32).T.astype(BF)

    for yy in range(4):
        acc[...] = jnp.zeros_like(acc)
        mec[...] = jnp.zeros_like(mec)
        lhs12 = g12t[16 * yy : 16 * yy + 16]

        def wstep(gg, carry):
            g = 3 * yy + gg
            main = ghb[1, :, 1:15, :, lanes_of(g)].reshape(ROWS, 128)
            lhs = jnp.concatenate([main.astype(F32).T.astype(BF), lhs12], axis=0)
            a = tap_concat(xb, lanes_of(g), False, ex[:, pl.ds(128 * yy, 128)])
            r = dot(lhs, a)
            for tap in range(9):
                x, pos = piece_of(gg * 9 + tap)
                blk = r[0:128, tap * 128 : tap * 128 + 128].astype(BF)
                at = pl.ds(pl.multiple_of(pos * 64, 64), 64)
                st[0, yy, x, at, :] = blk[0:64]
                st[1, x, yy, at, :] = blk[64:128]
            rowsel = (lax.broadcasted_iota(jnp.int32, (16, 1152), 0) // 4) == gg
            mec[...] += jnp.where(rowsel, r[128:144, 0:1152], 0.0)
            lane = lane_iota(144)
            lanesel = (lane >= 36 * gg) & (lane < 36 * gg + 36)
            rowsel2 = lax.broadcasted_iota(jnp.int32, (144, 128), 0)
            rowsel2 = (rowsel2 < 128) | (rowsel2 // 4 == 32 + gg)
            acc[0:144, :] += jnp.where(lanesel & rowsel2, r[:, 1152:1280], 0.0)
            return carry

        lax.fori_loop(0, 3, wstep, 0)
        blocks = [mec[:, 128 * tap : 128 * tap + 128].astype(BF) for tap in range(9)]
        eb = acc[0:144, :].astype(BF)
        zeros = jnp.zeros((64, 128), BF)
        for x in range(3):
            for k in range(3):
                st[0, yy, x, 448 + 16 * k : 464 + 16 * k, :] = blocks[3 * x + k]
            st[1, x, yy, 448:496, :] = eb[48 * x : 48 * x + 48]
            st[0, yy, x, 496:512, :] = zeros[0:16]
            st[1, x, yy, 496:512, :] = zeros[0:16]
        for h in range(2):
            st[h, (3 if h else yy), (yy if h else 3), 384:448, :] = zeros
            st[h, (3 if h else yy), (yy if h else 3), 448:512, :] = zeros

    tr_in = jnp.concatenate([me[128 * tap : 128 * tap + 128] for tap in range(9)], axis=1)
    tr[...] = dot(tr_in, ry[...]).astype(BF)
    tot[:, 1536:1664] = gs[:, 1536:1664]

    for yy in range(4):
        wt[128:256, :] = jnp.zeros((128, 1280), BF)

        def bstep(gg, carry):
            g = 3 * yy + gg
            for tap in range(9):
                wt[0:128, 128 * tap : 128 * tap + 128] = bm[g, 128 * tap : 128 * tap + 128, :]
            lane = lane_iota(128)
            lanesel = (lane >= 36 * gg) & (lane < 36 * gg + 36)
            wt[0:128, 1152:1280] = jnp.where(lanesel, tr[:, 128 * yy : 128 * yy + 128].astype(F32), 0.0).astype(BF)
            tails = ta[g].reshape(192, 128)
            bl = dot(selb[0, gg], tails).astype(BF)
            be = dot(selb[1, gg], tails)
            low = jnp.zeros((16, 128), F32)
            lane = lane_iota(16)
            for tap in range(9):
                wt[128 + 16 * yy : 144 + 16 * yy, 128 * tap : 128 * tap + 128] = bl[16 * tap : 16 * tap + 16]
                low = jnp.where((lane // 4) == 9 * gg + tap, be[16 * tap : 16 * tap + 16], low)
            wt[128 + 16 * yy : 144 + 16 * yy, 1152:1280] = low.astype(BF)
            a = tap_concat(ghb, lanes_of(g), True, eg[:, pl.ds(128 * yy, 128)])
            r = dot(a, wt[...], ((1,), (1,)))
            tot[:, lanes_of(g)] = gs[:, lanes_of(g)] + r[:, :128]
            tot[:, 1536:1664] += r[:, 128:]
            return carry

        lax.fori_loop(0, 3, bstep, 0)
    permute_out(lambda g: tot[:, lanes_of(g)].astype(BF), pg, ig_ref, on)


def back(hid, sums, gsum, par, gs, ga, xb, ex, bm, ta, me, c):
    return pl.pallas_call(
        back_body,
        in_specs=[vspec()] * 14,
        out_specs=[vspec()] * 2,
        out_shape=[
            struct((2, 14, 14, 1584), BF),
            struct((2, 4, 4, 512, 128), BF),
        ],
        scratch_shapes=[
            VM((3, 2, 16, 16, LANES), BF),
            VM((ROWS, 512), BF),
            VM((128, 512), BF),
            VM((256, 1280), BF),
            VM((ROWS, LANES), F32),
            VM((ROWS, 128), F32),
            VM((28, 16, LANES), BF),
            VM((16, 1152), F32),
        ],
        compiler_params=pltpu.CompilerParams(vmem_limit_bytes=VLIM),
        name="back",
    )(hid, sums, gsum, par, gs, ga, xb, ex, bm, ta, me, c["pg"], c["ry"], c["selb"])


def fin_constants():
    q_i = np.zeros((27, 256, 136), np.float32)
    q_o = np.zeros((3, 144, GW), np.float32)
    for gg in range(3):
        for a in range(4):
            for l in range(32):
                q_o[gg, 32 * a + l, 33 * a + l] = 1
                for tap in range(9):
                    q_i[gg * 9 + tap, 32 * a + l, 33 * a + l] = 1
            q_o[gg, 128 + 4 * gg + a, 33 * a + 32] = 1
            for tap in range(9):
                q_i[gg * 9 + tap, 128 + 36 * gg + 4 * tap + a, 33 * a + 32] = 1
    return jnp.asarray(q_i, BF), jnp.asarray(q_o, BF)


def fin_body(pos, h_ref, q_i, q_o, out_ref):
    b0 = pos[0]
    for k in range(3):
        b = b0 + k
        x, p = piece_of(b)
        tap = b % 9
        gg = b // 9
        at = pl.ds(pl.multiple_of(p * 64, 64), 64)
        main = jnp.concatenate([h_ref[0, x, at, :], h_ref[1, x, at, :]], axis=0)
        mrow = pl.ds(pl.multiple_of(448 + 16 * (tap % 3), 16), 16)
        me = h_ref[0, tap // 3, mrow, :]
        em = jnp.concatenate([h_ref[1, j, 448:496, :] for j in range(3)], axis=0)
        left = jnp.concatenate([main, me], axis=0)
        full = jnp.concatenate([left, em], axis=1)
        t1 = dot(full, q_i[b]).astype(BF)
        t2 = dot(t1, q_o[gg], ((0,), (0,)))
        out_ref[pl.ds(132 * k, 132), :] = t2[0:132]


def fin(pos, h):
    q_i, q_o = fin_constants()
    return pl.pallas_call(
        fin_body,
        in_specs=[sspec()] + [vspec()] * 3,
        out_specs=vspec(),
        out_shape=struct((396, GW), F32),
        compiler_params=pltpu.CompilerParams(vmem_limit_bytes=VLIM),
        name="fin",
    )(pos, h, q_i, q_o)


def channels_in(v):
    r = v.reshape(4, 3, 4, 33)
    main = r[..., :32].reshape(1536)
    extra = jnp.pad(r[..., 32].reshape(4, 12), ((0, 0), (0, 4))).reshape(64)
    return jnp.concatenate([main, extra, jnp.zeros((64,), v.dtype)])


def channels_out(v):
    main = v[:1536].reshape(4, 3, 4, 32)
    extra = v[1536:1600].reshape(4, 16)[:, :12].reshape(4, 3, 4, 1)
    return jnp.concatenate([main, extra], axis=-1).reshape(1584)
MESH = pl.DeviceIdType.MESH


def place():
    dp = lax.axis_index("dp")
    s = lax.axis_index("shard")
    return (s // 2) % 4, s // 16, dp * 2 + (s // 8) % 2, s % 2


def device(x, y, z, c):
    return (z // 2, y * 16 + (z % 2) * 8 + x * 2 + c)


def greet(devices):
    barrier = pltpu.get_barrier_semaphore()
    for d in devices:
        pl.semaphore_signal(barrier, inc=1, device_id=d, device_id_type=MESH)
    pl.semaphore_wait(barrier, len(devices))


def send(src, dst, send_sem, recv_sem, to):
    copy = pltpu.make_async_remote_copy(
        src_ref=src, dst_ref=dst, send_sem=send_sem, recv_sem=recv_sem,
        device_id=to, device_id_type=MESH,
    )
    copy.start()
    return copy


def remote_params(number):
    return pltpu.CompilerParams(
        collective_id=number, has_side_effects=True, vmem_limit_bytes=VLIM
    )


DMA = pltpu.SemaphoreType.DMA


def gather_body(pay, out, s_sib, r_sib, s_z, r_z, s_u, r_u, s_v, r_v, s_d, r_d):
    x, y, z, c = place()
    zl = z % 2
    oz = 1 - zl
    u = x * (1 - c) + y * c
    v = y * (1 - c) + x * c

    def at_u(k):
        k = (u + k) % 4
        return device(k * (1 - c) + x * c, y * (1 - c) + k * c, z, c)

    def at_v(k):
        k = (v + k) % 4
        return device(x * (1 - c) + k * c, k * (1 - c) + y * c, z, c)

    sib = device(x, y, z, 1 - c)
    zp, zm = device(x, y, (z + 1) % 8, c), device(x, y, (z + 7) % 8, c)
    greet([sib, zp, zm, at_u(1), at_u(3), at_v(1), at_v(3)])
    sends = []

    mine = out.at[c, v, u, zl, c]
    other = out.at[1 - c, u, v, zl, c]
    mine[...] = pay[pl.ds(2 * c, 2)]
    other[...] = pay[pl.ds(2 - 2 * c, 2)]
    sib_copy = send(other, other, s_sib.at[0], r_sib.at[0], sib)
    sends.append(sib_copy)
    sends.append(send(mine, mine, s_d.at[32], r_d.at[32], sib))
    sib_copy.wait_recv()

    a, b = out.at[c, v, u, zl, 0], out.at[c, v, u, zl, 1]
    z0 = send(a, a, s_z.at[0], r_z.at[0], zp)
    z1 = send(b, b, s_z.at[1], r_z.at[1], zm)
    sends += [z0, z1]

    def chunk(i, j, zz):
        return out.at[c, (v + i) % 4, (u + j) % 4, zz]

    def spread_u(n, zz):
        k = chunk(0, 0, zz)
        return [send(k, k, s_u.at[n, 0], r_u.at[n, 0], at_u(1)),
                send(k, k, s_u.at[n, 1], r_u.at[n, 1], at_u(3))]

    def spread_v(n, k):
        return [send(k, k, s_v.at[n, 0], r_v.at[n, 0], at_v(1)),
                send(k, k, s_v.at[n, 1], r_v.at[n, 1], at_v(3))]

    def pass_on(n, k):
        sends.append(send(k, k, s_d.at[n], r_d.at[n], sib))

    order = [(0, zl), (0, oz), (3, zl), (1, zl), (3, oz), (1, oz), (2, zl), (2, oz)]
    ring_u, ring_v = {}, {}

    ring_u[0] = spread_u(0, zl)
    ring_v[0] = spread_v(0, chunk(0, 0, zl))
    z0.wait_recv()
    z1.wait_recv()
    ring_u[1] = spread_u(1, oz)
    ring_v[1] = spread_v(1, chunk(0, 0, oz))
    pass_on(1, chunk(0, 0, oz))
    sends += ring_u[0] + ring_u[1] + ring_v[0] + ring_v[1]
    half_u = {}
    for n, zz in ((0, zl), (1, oz)):
        ring_u[n][0].wait_recv()
        k = chunk(0, 3, zz)
        h0 = send(k.at[0], k.at[0], s_u.at[n, 2], r_u.at[n, 2], at_u(1))
        ring_v[2 + 2 * n] = spread_v(2 + 2 * n, k)
        pass_on(2 + 2 * n, k)
        ring_u[n][1].wait_recv()
        k = chunk(0, 1, zz)
        h1 = send(k.at[1], k.at[1], s_u.at[n, 3], r_u.at[n, 3], at_u(3))
        ring_v[3 + 2 * n] = spread_v(3 + 2 * n, k)
        pass_on(3 + 2 * n, k)
        sends += [h0, h1] + ring_v[2 + 2 * n] + ring_v[3 + 2 * n]
        half_u[n] = (h0, h1)
    for n, zz in ((0, zl), (1, oz)):
        half_u[n][0].wait_recv()
        half_u[n][1].wait_recv()
        k = chunk(0, 2, zz)
        ring_v[6 + n] = spread_v(6 + n, k)
        pass_on(6 + n, k)
        sends += ring_v[6 + n]
    half_v = {}
    for n, (j, zz) in enumerate(order):
        ring_v[n][0].wait_recv()
        k = chunk(3, j, zz)
        h0 = send(k.at[0], k.at[0], s_v.at[n, 2], r_v.at[n, 2], at_v(1))
        pass_on(8 + n, k)
        ring_v[n][1].wait_recv()
        k = chunk(1, j, zz)
        h1 = send(k.at[1], k.at[1], s_v.at[n, 3], r_v.at[n, 3], at_v(3))
        pass_on(16 + n, k)
        sends += [h0, h1]
        half_v[n] = (h0, h1)
    for n, (j, zz) in enumerate(order):
        half_v[n][0].wait_recv()
        half_v[n][1].wait_recv()
        pass_on(24 + n, chunk(2, j, zz))
    for copy in sends:
        copy.wait_send()
    for n in list(range(1, 32)):
        k = out.at[1 - c, 0, 0, 0]
        pltpu.make_async_remote_copy(
            src_ref=k, dst_ref=k, send_sem=s_d.at[n], recv_sem=r_d.at[n],
            device_id=sib, device_id_type=MESH,
        ).wait_recv()
    sends[1].wait_recv()


def gather_tiles(pay):
    return pl.pallas_call(
        gather_body,
        in_specs=[vspec()],
        out_specs=vspec(),
        out_shape=struct((2, 4, 4, 2, 2, 2, 112, 128), BF),
        scratch_shapes=[
            DMA((1,)), DMA((1,)), DMA((2,)), DMA((2,)), DMA((2, 4)), DMA((2, 4)),
            DMA((8, 4)), DMA((8, 4)), DMA((33,)), DMA((33,)),
        ],
        compiler_params=remote_params(1),
        name="gather_tiles",
    )(pay)


def partners(x, y, z, c):
    out = [device(x, y, z, 1 - c)]
    out += [device((x + r) % 4, y, z, c) for r in range(1, 4)]
    out += [device(x, (y + r) % 4, z, c) for r in range(1, 4)]
    out += [device(x, y, (z + r) % 8, c) for r in range(1, 8)]
    return out


def reduce_body(v_ref, out_ref, b0, b1, b2, b3, ssem, rsem):
    x, y, z, c = place()
    greet(partners(x, y, z, c))
    stages = [
        (b0, 2, c, lambda q: device(x, y, z, q)),
        (b1, 4, x, lambda q: device(q, y, z, c)),
        (b2, 4, y, lambda q: device(x, q, z, c)),
        (b3, 8, z, lambda q: device(x, y, q, c)),
    ]
    value = v_ref[...]
    base = 0
    sends = []
    for buf, n, p, dev in stages:
        buf[p] = value
        copies = [
            send(buf.at[p], buf.at[p], ssem.at[base + r], rsem.at[base + r], dev((p + r) % n))
            for r in range(1, n)
        ]
        for copy in copies:
            copy.wait_recv()
        value = buf[0]
        for k in range(1, n):
            value = value + buf[k]
        base += n
        sends += copies
    out_ref[...] = value
    for copy in sends:
        copy.wait_send()


def reduce_sums(v, number):
    return pl.pallas_call(
        reduce_body,
        in_specs=[vspec()],
        out_specs=vspec(),
        out_shape=struct((2, LANES), F32),
        scratch_shapes=[VM((n, 2, LANES), F32) for n in (2, 4, 4, 8)]
        + [DMA((18,)), DMA((18,))],
        compiler_params=remote_params(number),
        name="reduce_sums",
    )(v)


def scatter_body(st, out, r0, cur, r1, cur2, r2, cur3, r3, ss, rs):
    x, y, z, c = place()
    greet(partners(x, y, z, c))
    u = x * (1 - c) + y * c
    v = y * (1 - c) + x * c
    sib = device(x, y, z, 1 - c)

    def at_u(k):
        return device(k * (1 - c) + x * c, y * (1 - c) + k * c, z, c)

    def at_v(k):
        return device(x * (1 - c) + k * c, k * (1 - c) + y * c, z, c)

    sends = []
    first = []
    for r in range(4):
        q = (v + 1 + r) % 4
        first.append(send(st.at[1 - c, r], r0.at[r], ss.at[r], rs.at[r], sib))
    sends += first
    for r in range(4):
        first[r].wait_recv()

        def add(k, carry, r=r):
            row = pl.ds(pl.multiple_of(k * 64, 64), 64)
            for j in range(4):
                cur[r, j, row, :] = (st[c, r, j, row, :].astype(F32) + r0[r, j, row, :].astype(F32)).astype(BF)
            return carry

        lax.fori_loop(0, 8, add, 0)
    second = []
    for r in range(1, 4):
        q = (v + r) % 4
        second.append(send(cur.at[q], r1.at[r - 1], ss.at[3 + r], rs.at[3 + r], at_v(q)))
    sends += second
    for copy in second:
        copy.wait_recv()

    def add1(k, carry):
        row = pl.ds(pl.multiple_of(k * 64, 64), 64)
        for j in range(4):
            total = cur[v, j, row, :].astype(F32)
            for r in range(3):
                total = total + r1[r, j, row, :].astype(F32)
            cur2[j, row, :] = total.astype(BF)
        return carry

    lax.fori_loop(0, 8, add1, 0)
    third = []
    for r in range(1, 4):
        q = (u + r) % 4
        third.append(send(cur2.at[q], r2.at[r - 1], ss.at[6 + r], rs.at[6 + r], at_u(q)))
    sends += third
    for copy in third:
        copy.wait_recv()

    def add2(k, carry):
        row = pl.ds(pl.multiple_of(k * 64, 64), 64)
        total = cur2[u, row, :].astype(F32)
        for r in range(3):
            total = total + r2[r, row, :].astype(F32)
        cur3[k] = total.astype(BF)
        return carry

    lax.fori_loop(0, 8, add2, 0)
    fourth = []
    for r in range(1, 8):
        q = (z + r) % 8
        fourth.append(send(cur3.at[q], r3.at[r - 1], ss.at[9 + r], rs.at[9 + r], device(x, y, q, c)))
    sends += fourth
    for copy in fourth:
        copy.wait_recv()
    total = cur3[z].astype(F32)
    for r in range(7):
        total = total + r3[r].astype(F32)
    out[c, x, z] = total.astype(BF)
    fifth = []
    here = out.at[c, x, z]
    for r in range(1, 8):
        q = (z + r) % 8
        fifth.append(send(here, here, ss.at[16 + r], rs.at[16 + r], device(x, y, q, c)))
    sends += fifth
    for copy in fifth:
        copy.wait_recv()
    sixth = []
    here = out.at[c, x]
    for r in range(1, 4):
        q = (x + r) % 4
        sixth.append(send(here, here, ss.at[23 + r], rs.at[23 + r], device(q, y, z, c)))
    sends += sixth
    for copy in sixth:
        copy.wait_recv()
    here = out.at[c]
    last = send(here, here, ss.at[27], rs.at[27], sib)
    last.wait_recv()
    sends.append(last)
    for copy in sends:
        copy.wait_send()


def scatter_grad(st):
    return pl.pallas_call(
        scatter_body,
        in_specs=[vspec()],
        out_specs=vspec(),
        out_shape=struct((2, 4, 8, 64, 128), BF),
        scratch_shapes=[
            VM((4, 4, 512, 128), BF), VM((4, 4, 512, 128), BF),
            VM((3, 4, 512, 128), BF), VM((4, 512, 128), BF),
            VM((3, 512, 128), BF), VM((8, 64, 128), BF), VM((7, 64, 128), BF),
            DMA((28,)), DMA((28,)),
        ],
        compiler_params=remote_params(4),
        name="scatter_grad",
    )(st)


def tile_rows(tile_counts, owner_order):
    run_end = jnp.cumsum(tile_counts)
    run_start = run_end - tile_counts
    tile_ids = jnp.arange(144, dtype=jnp.int32)
    rank_of = jnp.sum((run_end[None, :] <= tile_ids[:, None]).astype(jnp.int32), axis=1)
    onehot = (rank_of[:, None] == jnp.arange(64, dtype=jnp.int32)[None, :]).astype(jnp.int32)
    s = jnp.sum(onehot * owner_order[None, :], axis=1)
    j = tile_ids - jnp.sum(onehot * run_start[None, :], axis=1)
    y, zl, x, core = s // 16, (s // 8) % 2, (s // 2) % 4, s % 2
    vu = jnp.where(j < 2, y * 4 + x, x * 4 + y)
    return (j // 2) * 128 + vu * 8 + zl * 4 + core * 2 + j % 2


def local(block_input, upstream, kernel_tiles, tile_counts, owner_order, gain, bias):
    c = constants()
    idx = tile_rows(tile_counts, owner_order)
    par = jnp.stack([channels_in(gain), channels_in(bias)])
    gathered = gather_tiles(prep(kernel_tiles.reshape(4, 99, 132))).reshape(256, 112, 128)
    xb, ex, hid, bm, ta, me, sums = fwd(idx, block_input, gathered, c)
    sums = reduce_sums(sums, 2)
    block_out, gs, ga, gsum = norm(upstream, xb, hid, sums, par, c)
    gsum = reduce_sums(gsum, 3)
    input_grad, st = back(hid, sums, gsum, par, gs, ga, xb, ex, bm, ta, me, c)
    h = scatter_grad(st).reshape(2, 4, 512, 128)
    sp = lax.axis_index("shard") % 16
    b0 = jnp.minimum((sp * 29403) // 17424, 24)
    flat = fin(b0.reshape(1), h).reshape(-1)
    kernel_grad = lax.dynamic_slice(flat, (sp * 29403 - b0 * 17424,), (29403,))
    return (block_out, input_grad, kernel_grad, channels_out(gsum[0]), channels_out(gsum[1]))


def solution(mesh):
    return jax.shard_map(
        local,
        mesh=mesh,
        in_specs=(
            P(("dp", "shard"), None, None, None),
            P(("dp", "shard"), None, None, None),
            P("shard", None),
            P(),
            P(),
            P(),
            P(),
        ),
        out_specs=(
            P(("dp", "shard"), None, None, None),
            P(("dp", "shard"), None, None, None),
            P("shard"),
            P(),
            P(),
        ),
        check_vma=False,
    )
```

time: 980 us -> 217 us (0.22); the launches traced: 961 us -> 217 us
  blocking collectives: 487 us -> 0 us
  local copies, waits for them, and re-layouts: 410 us -> 17.3 us
  Pallas kernels: 0 us -> 197 us
  matrix products: 34.7 us -> 0 us
  between operations: 15.3 us -> 0.81 us
  other arithmetic: 13.6 us -> 1.79 us
    unnamed x1 -> x0, blocking collectives: 318 us -> none
    another operation x39 -> x6, local copies, waits for them, and re-layouts: 255 us -> 0.28 us  [the longest x2 0.17 us: channels_in(): extra = jnp.pad(r[..., 32].reshape(4, 12), ((0, 0), (0, 4))).reshape(64)]
    pallas_call x0 -> x9, Pallas kernels: none -> 197 us  [the longest x1 53 us: scatter_grad(): pl.pallas_call(scatter_body, in_specs=[vspec()], out_specs=vspec(), out_s...]
    psum x3 -> x0, blocking collectives: 169 us -> none  [the longest x1 81.6 us: local(): lax.psum((jnp.sum(values, axis=(0, 1, 2)), jnp.sum(values * values, axis=...]
    reshape x4 -> x16, local copies, waits for them, and re-layouts: 46.6 us -> 4.83 us  [the longest x2 1.46 us: channels_out(): return jnp.concatenate([main, extra], axis=-1).reshape(1584)]
    dot_general x3 -> x0, matrix products: 34.7 us -> none  [the longest x1 13.3 us: local(): jnp.einsum('rgti,rgo->gtio', input_columns, grad_rows, preferred_element_...]
    unnamed x74 -> x18, local copies, waits for them, and re-layouts: 44.3 us -> 10.9 us
    slice x10 -> x4, local copies, waits for them, and re-layouts: 31.1 us -> 0.4 us  [the longest x2 0.34 us: channels_in(): extra = jnp.pad(r[..., 32].reshape(4, 12), ((0, 0), (0, 4))).reshape(64)]
  transfers between devices with their start and end apart: 1 -> 0, of which waited for: 0 -> 0; matrix products, arithmetic and copies ran while one was open for 18% -> 0% of each run, Pallas kernels for 0% -> 0%
where the time goes in v1:
time: 217 us
  Pallas kernels  197 us (91%)
  local copies, waits for them, and re-layouts  17.3 us (8%)
    pallas_call x1, Pallas kernels, scatter_grad(): pl.pallas_call(scatter_body, in_specs=[vspec()], out_specs=vspec(), out_s...  53 us
    pallas_call x1, Pallas kernels, gather_tiles(): pl.pallas_call(gather_body, in_specs=[vspec()], out_specs=vspec(), out_sh...  39.2 us
    pallas_call x2, Pallas kernels, reduce_sums(): pl.pallas_call(reduce_body, in_specs=[vspec()], out_specs=vspec(), out_sh...  33.2 us
    pallas_call x1, Pallas kernels, back(): pl.pallas_call(back_body, in_specs=[vspec()] * 14, out_specs=[vspec()] *...  28.4 us
    pallas_call x1, Pallas kernels, fwd(): pl.pallas_call(fwd_body, in_specs=[sspec()] + [vspec()] * 6, out_specs=[v...  21.4 us
    pallas_call x1, Pallas kernels, norm(): pl.pallas_call(norm_body, in_specs=[vspec()] * 6, out_specs=[vspec()] * 4...  15.7 us
    unnamed x18, local copies, waits for them, and re-layouts  10.9 us

profile of v1, /device:TPU:1, one launch (start us, length us, event | category | flops | bytes accessed | tf_op | source)
XLA Modules:
  0.0 217.1 jit_solution(10447181322022279655)
XLA Ops:
  0.6 0.0 copy-start.5
  0.6 0.0 copy-start.6
  0.7 0.0 copy-start
  0.7 2.7 %copy.41.up_ref = bf16[2,14,14,1584]{3,2,1,0:T(8,128)(2,1)} copy(bf16[2,14,14,1584]{3,0,2,1:T(2,128)(2,1)} %param.21) | data formatting | bytes 2483712 | tf_op args[1]
  3.3 0.0 copy-start.2
  3.4 0.0 copy-done.5
  3.4 0.1 copy.39
  3.4 0.1 reduce-window.8
  3.5 0.1 reduce
  3.7 0.1 convert_reduce_fusion
  3.8 0.0 copy-done.6
  3.8 0.1 select_reduce_fusion.1
  3.9 0.6 fusion.4.idx
  4.5 0.0 copy-done
  4.5 1.3 copy.40.x_ref
  5.8 0.0 copy-done.2
  5.8 1.0 reshape.103.tile_ref
  6.8 2.3 %prep.1.pay = bf16[4,112,128]{2,1,0:T(8,128)(2,1)} custom-call(bf16[4,99,132]{2,1,0:T(8,128)(2,1)} %reshape.103.tile_ref, bf16[132,128]{1,0:T(8,128)(2,1)} %constant.148.clone.cs, bf16[132,112]{1,0:T(8,128)(2,1)} %constant.149.clone.cse, bf16[132,128]{1,0:T(8,128)(2,1)} %constant.150.clone.csee, bf16[112,99]{1,0:T(8,128)(2,1)} %constant.151.clone.rs, ...), custom_call_target="tpu_custom_call" | custom-call | tf_op jit(solution)/shard_map/prep/pallas_call | solution.py:95
  9.1 39.2 %gather_tiles.1 = bf16[2,4,4,2,2,2,112,128]{7,6,5,4,3,2,1,0:T(8,128)(2,1)} custom-call(bf16[4,112,128]{2,1,0:T(8,128)(2,1)} %prep.1.pay), custom_call_target="tpu_custom_call" | custom-call | tf_op jit(solution)/shard_map/gather_tiles/pallas_call | solution.py:665
  48.3 0.0 copy-start.3
  48.3 0.0 copy-start.4
  48.3 21.4 %fwd.1 = (bf16[3,2,16,16,1664]{4,3,2,1,0:T(8,128)(2,1)}, bf16[448,512]{1,0:T(8,128)(2,1)}, bf16[448,1664]{1,0:T(8,128)(2,1)}, bf16[12,1152,128]{2,1,0:T(8,128)(2...) custom-call(s32[144]{0:T(256)} %fusion.4.idx, ...), custom_call_target="tpu_custom_call" | custom-call | tf_op jit(solution)/shard_map/fwd/pallas_call | solution.py:236
  69.8 15.5 %reduce_sums.2.sums = f32[2,1664]{1,0:T(2,128)} custom-call(f32[2,1664]{1,0:T(2,128)} %get-tuple-element.20.v_ref), custom_call_target="tpu_custom_call" | custom-call | tf_op jit(solution)/shard_map/reduce_sums/pallas_call | solution.py:718
  85.2 0.0 copy-done.3
  85.3 0.1 reshape.108
  85.4 0.1 reshape.109
  85.5 0.2 slice_reduce_fusion
  85.6 0.1 reshape_squeeze.7
  85.7 0.1 reshape.110
  85.8 0.1 concatenate.13
  85.9 0.0 copy-done.4
  85.9 0.1 reshape.105
  86.0 0.1 reshape.106
  86.1 0.2 slice_reduce_fusion.1
  86.3 0.1 reshape_squeeze.6
  86.4 0.1 reshape.107
  86.5 0.1 concatenate.12
  86.6 0.6 pad_maximum_fusion.2.par
  87.2 15.7 %norm.1 = (bf16[2,14,14,1584]{3,2,1,0:T(8,128)(2,1)}, f32[448,1664]{1,0:T(8,128)}, f32[448,1664]{1,0:T(8,128)}, f32[2,1664]{1,0:T(2,128)}) custom-call(bf16[2,14,14,1584]{3,2,1,0:T(8,128)(2,1)} %copy.41.up_ref, bf16[3,2,16,16,1664]{4,3,2,1,0:T(8,128)(2,1)} %get-tuple-element.18.xb, bf16[448,1664]{1,0:T(8,128)(2,1)} %get-tuple-element.19.hid, ...), custom_call_target="tpu_custom_call" | custom-call | tf_op jit(solution)/shard_map/norm/pallas_call | solution.py:306
  102.9 3.4 %copy.44 = bf16[2,14,14,1584]{3,0,2,1:T(2,128)(2,1)} copy(bf16[2,14,14,1584]{3,2,1,0:T(8,128)(2,1)} %get-tuple-element.41) | data formatting | bytes 2483712
  106.4 17.8 %reduce_sums.3.gsum = f32[2,1664]{1,0:T(2,128)} custom-call(f32[2,1664]{1,0:T(2,128)} %get-tuple-element.22.v_ref), custom_call_target="tpu_custom_call" | custom-call | tf_op jit(solution)/shard_map/reduce_sums/pallas_call | solution.py:718
  124.1 28.4 %back.1 = (bf16[2,14,14,1584]{3,2,1,0:T(8,128)(2,1)}, bf16[2,4,4,512,128]{4,3,2,1,0:T(8,128)(2,1)}) custom-call(bf16[448,1664]{1,0:T(8,128)(2,1)} %get-tuple-element.19.hid, f32[2,1664]{1,0:T(2,128)} %reduce_sums.2.sums, f32[2,1664]{1,0:T(2,128)} %reduce_sums.3.gsum, f32[2,1664]{1,0:T(2,128)} %pad_maximum_fusion.2.par, f32[448,1664]{1,0:T(8,128)} %get-tuple-element.23.gs, ...), custom_call_target="tpu_custom_call" | custom-call | tf_op jit(solution)/shard_map/back/pallas_call | solution.py:438
  152.6 3.4 %copy.45 = bf16[2,14,14,1584]{3,0,2,1:T(2,128)(2,1)} copy(bf16[2,14,14,1584]{3,2,1,0:T(8,128)(2,1)} %get-tuple-element.42) | data formatting | bytes 2483712
  156.0 53.0 %scatter_grad.1 = bf16[2,4,8,64,128]{4,3,2,1,0:T(8,128)(2,1)} custom-call(bf16[2,4,4,512,128]{4,3,2,1,0:T(8,128)(2,1)} %get-tuple-element.30.st), custom_call_target="tpu_custom_call" | custom-call | tf_op jit(solution)/shard_map/scatter_grad/pallas_call | solution.py:830
  209.1 0.0 copy-start.1
  209.1 3.8 %fin.1 = f32[396,132]{1,0:T(8,128)} custom-call(s32[1]{0:T(128)} %bitcast.2.pos, bf16[2,4,512,128]{3,2,1,0:T(8,128)(2,1)} %bitcast.9, bf16[27,256,136]{2,1,0:T(8,128)(2,1)} %constant.154.clone.q_i, bf16[3,144,132]{2,1,0:T(8,128)(2,1)} %constant.155.clone.q_o), custom_call_target="tpu_custom_call" | custom-call | tf_op jit(solution)/shard_map/fin/pallas_call | solution.py:497
  212.8 1.3 reshape.113
  214.1 0.8 dynamic_slice.3
  214.9 0.0 copy-done.1
  214.9 0.1 reshape.115
  215.0 0.1 reshape.122
  215.1 0.1 reshape.114
  215.2 0.1 pad_maximum_fusion
  215.3 0.7 reshape.117
  216.0 0.1 reshape.119
  216.1 0.1 reshape.123
  216.2 0.1 reshape.118
  216.3 0.1 pad_maximum_fusion.1
  216.4 0.7 reshape.121
  (8 shorter events, 0.1 us)
Async XLA Ops:
  0.6 2.7 %copy-start.5 = (s32[64]{0:T(128)S(1)}, s32[64]{0:T(128)}, u32[]{:S(2)}) copy-start(s32[64]{0:T(128)} %param.23) | copy-start | bytes 772
  0.6 3.1 %copy-start.6 = (s32[64]{0:T(128)S(1)}, s32[64]{0:T(128)}, u32[]{:S(2)}) copy-start(s32[64]{0:T(128)} %param.24) | copy-start | bytes 772
  0.7 3.8 %copy-start = (bf16[2,14,14,1584]{3,0,2,1:T(2,128)(2,1)S(1)}, bf16[2,14,14,1584]{3,0,2,1:T(2,128)(2,1)}, u32[]{:S(2)}) copy-start(bf16[2,14,14,1584]{3,0,2,1:T(2,128)(2,1)} %param.20) | copy-start | bytes 3725572
  3.3 2.4 %copy-start.2 = (bf16[4,13068]{1,0:T(4,128)(2,1)S(1)}, bf16[4,13068]{1,0:T(4,128)(2,1)}, u32[]{:S(2)}) copy-start(bf16[4,13068]{1,0:T(4,128)(2,1)} %param.22) | copy-start | bytes 313636
  48.3 36.9 %copy-start.3 = (f32[1584]{0:T(1024)S(1)}, f32[1584]{0:T(1024)}, u32[]{:S(2)}) copy-start(f32[1584]{0:T(1024)} %param.26) | copy-start | bytes 19012
  48.3 37.6 %copy-start.4 = (f32[1584]{0:T(1024)S(1)}, f32[1584]{0:T(1024)}, u32[]{:S(2)}) copy-start(f32[1584]{0:T(1024)} %param.25) | copy-start | bytes 19012
  209.1 5.8 %copy-start.1 = (f32[2,1664]{1,0:T(2,128)S(1)}, f32[2,1664]{1,0:T(2,128)}, u32[]{:S(2)}) copy-start(f32[2,1664]{1,0:T(2,128)} %reduce_sums.3.gsum) | copy-start | bytes 39940

commit v2 on v0

v2 whole, which is shorter than its diff:
```python
import numpy as np
import jax
import jax.numpy as jnp
from jax import lax
from jax.experimental import pallas as pl
from jax.experimental.pallas import tpu as pltpu
from jax.sharding import PartitionSpec as P

GROUPS = 12
GW = 132
ROWS = 448
LANES = 1664
BF = jnp.bfloat16
F32 = jnp.float32
EPSILON = 1e-05
TOTAL = 100352
VLIM = 60 * 1024 * 1024


def extra_lane(g, a):
    return 16 * (g // 3) + 4 * (g % 3) + a


def constants():
    pg = np.zeros((GROUPS, 256, 256), np.float32)
    for g in range(GROUPS):
        for j in range(GW):
            a, l = j // 33, j % 33
            pg[g, 4 * g + j, 32 * a + l if l < 32 else 128 + extra_lane(g, a)] = 1
    ry = np.zeros((9, 128, 4, 128), np.float32)
    for g in range(GROUPS):
        for tap in range(9):
            for a in range(4):
                ry[tap, extra_lane(g, a), g // 3, 36 * (g % 3) + 4 * tap + a] = 1
    selm = np.zeros((GROUPS, 16, 128), np.float32)
    for g in range(GROUPS):
        for a in range(4):
            selm[g, 3 + a, extra_lane(g, a)] = 1
    sele = np.zeros((2, 3, 128, 12, 16), np.float32)
    selb = np.zeros((2, 3, 9, 16, 12, 16), np.float32)
    for gg in range(3):
        for u in range(36):
            q, j = u // 3, u % 3
            tap, a = u // 4, u % 4
            for kind, row in ((0, j), (1, 7 + j)):
                sele[kind, gg, 36 * gg + u, q, row] = 1
                selb[kind, gg, tap, 4 * gg + a, q, row] = 1
    bf = lambda v, *s: jnp.asarray(v.reshape(s), BF)
    return dict(
        pg=bf(pg, GROUPS, 256, 256),
        ry=bf(ry, 1152, 512),
        selm=bf(selm, 192, 128),
        sele=bf(sele, 2, 3, 128, 192),
        selb=bf(selb, 2, 3, 144, 192),
    )


def prep_constants():
    cs = np.zeros((GW, 128), np.float32)
    cse = np.zeros((GW, 112), np.float32)
    csee = np.zeros((GW, 128), np.float32)
    rs = np.zeros((112, 99), np.float32)
    rsm = np.zeros((99, 128), np.float32)
    rse = np.zeros((112, 99), np.float32)
    for a in range(4):
        for l in range(32):
            cs[33 * a + l, 32 * a + l] = 1
        cse[33 * a + 32, 99 + a] = 1
    for lane in range(128):
        csee[33 * (lane % 4) + 32, lane] = 1
    for j in range(3):
        for l in range(32):
            rs[32 * j + l, 33 * j + l] = 1
            rsm[33 * j + l, 32 * j + l] = 1
        rs[96 + j, 33 * j + 32] = 1
        rse[103 + j, 33 * j + 32] = 1
    return [jnp.asarray(v, BF) for v in (cs, cse, csee, rs, rsm, rse)]


def dot(a, b, dims=((1,), (0,))):
    return lax.dot_general(a, b, (dims, ((), ())), preferred_element_type=F32)


MESH = pl.DeviceIdType.MESH
DMA = pltpu.SemaphoreType.DMA
VM = pltpu.VMEM


def vspec():
    return pl.BlockSpec(memory_space=VM)


def struct(shape, dtype):
    return jax.ShapeDtypeStruct(shape, dtype)


def lanes_of(g, width=1):
    if isinstance(g, int):
        return pl.ds(g * 128, 128 * width)
    return pl.ds(pl.multiple_of(g * 128, 128), 128 * width)


def rows_at(start, size):
    if isinstance(start, int):
        return pl.ds(start, size)
    return pl.ds(pl.multiple_of(start, 16), size)


def lane_iota(rows):
    return lax.broadcasted_iota(jnp.int32, (rows, 128), 1)


def half_tanh(v):
    return 0.5 * jnp.tanh(0.5 * v) + 0.5


def place():
    dp = lax.axis_index("dp")
    s = lax.axis_index("shard")
    return (s // 2) % 4, s // 16, dp * 2 + (s // 8) % 2, s % 2


def device(x, y, z, c):
    return (z // 2, y * 16 + (z % 2) * 8 + x * 2 + c)


def send(src, dst, send_sem, recv_sem, to):
    copy = pltpu.make_async_remote_copy(
        src_ref=src, dst_ref=dst, send_sem=send_sem, recv_sem=recv_sem,
        device_id=to, device_id_type=MESH,
    )
    copy.start()
    return copy


def load_native(raw, xn):
    xn[...] = jnp.zeros_like(xn)
    for y in range(14):
        xn[y, 0:28, 0:1584] = raw[y].reshape(28, 1584)


def store_shifts(dst, main, lanes):
    for b in range(3):
        moved = main if b == 1 else pltpu.roll(main, (2 - 2 * b) % ROWS, 0)
        dst[b, 1:15, :, lanes] = moved.astype(BF).reshape(14, 32, 128)


def zero_borders(dst):
    zeros = jnp.zeros((3, 32, LANES), BF)
    dst[:, 0] = zeros
    dst[:, 15] = zeros


def tap_slice(src, tap, lanes, mirrored):
    a, b = tap // 3, tap % 3
    if mirrored:
        a, b = 2 - a, 2 - b
    return src[b, a : a + 14, :, lanes].reshape(ROWS, 128)


def tap_concat(src, lanes, mirrored, extra=None):
    pieces = [tap_slice(src, tap, lanes, mirrored) for tap in range(9)]
    if extra is not None:
        pieces.append(extra)
    return jnp.concatenate(pieces, axis=1)


def piece_of(b):
    s = {t: (b + 27 - t) // 27 for t in (3, 7, 10, 13, 17, 20, 24)}
    x = s[3] + s[7] + s[10] - 3 * s[13] + s[17] + s[20] + s[24]
    pos = b - 3 * s[3] - 4 * s[7] - 3 * s[10] - 3 * s[17] - 4 * s[20] - 4 * s[24]
    return x, pos


def fin_constants():
    q_m = np.zeros((128, 136), np.float32)
    q_o = np.zeros((3, 144, GW), np.float32)
    for a in range(4):
        for l in range(32):
            q_m[32 * a + l, 33 * a + l] = 1
            q_o[:, 32 * a + l, 33 * a + l] = 1
        for gg in range(3):
            q_o[gg, 128 + 4 * gg + a, 33 * a + 32] = 1
    return jnp.asarray(q_m, BF), jnp.asarray(q_o, BF)


IN_NAMES = (
    "idx", "tile", "cs", "cse", "csee", "rs", "rsm", "rse", "par",
    "pg", "ry", "selm", "sele", "selb", "qm", "qo", "x_hbm", "up_hbm",
)
OUT_NAMES = ("out_hbm", "ig_hbm", "kg", "gsum")


def scratch_list():
    sets = dict(
        pay=VM((4, 112, 128), BF),
        gat=VM((256, 112, 128), BF),
        xb=VM((3, 16, 32, LANES), BF),
        ghb=VM((3, 16, 32, LANES), BF),
        ex=VM((ROWS, 512), BF),
        eg=VM((ROWS, 512), BF),
        bm=VM((GROUPS, 1152, 128), BF),
        ta=VM((GROUPS, 12, 16, 128), BF),
        me=VM((1152, 128), BF),
        hid=VM((ROWS, LANES), BF),
        gs=VM((ROWS, LANES), F32),
        ga=VM((ROWS, LANES), F32),
        upp=VM((ROWS, LANES), BF),
        bo=VM((ROWS, LANES), BF),
        raw=VM((14, 14, 2, 1584), BF),
        raw2=VM((14, 14, 2, 1584), BF),
        xn=VM((14, 32, LANES), BF),
        acc=VM((ROWS, 128), F32),
        mec=VM((16, 1152), F32),
        bg=VM((1280, 256), BF),
        wt=VM((256, 1280), BF),
        tr=VM((128, 512), BF),
        g12t=VM((128, ROWS), BF),
        st=VM((2, 4, 4, 512, 128), BF),
        r0=VM((4, 4, 512, 128), BF),
        r1=VM((3, 4, 512, 128), BF),
        cur2=VM((4, 512, 128), BF),
        r2=VM((3, 512, 128), BF),
        cur3=VM((8, 64, 128), BF),
        r3=VM((7, 64, 128), BF),
        hh=VM((2, 4, 8, 64, 128), BF),
        sums=VM((2, LANES), F32),
        lsum=VM((2, LANES), F32),
        s_in=DMA((2,)),
        s_out=DMA((2,)),
        s_sib=DMA((1,)), r_sib=DMA((1,)),
        s_z=DMA((2,)), r_z=DMA((2,)),
        s_u=DMA((2, 4)), r_u=DMA((2, 4)),
        s_v=DMA((8, 4)), r_v=DMA((8, 4)),
        s_d=DMA((33,)), r_d=DMA((33,)),
        s_c=DMA((16,)), r_c=DMA((16,)),
        s_1=DMA((12,)), r_1=DMA((12,)),
        s_2=DMA((3,)), r_2=DMA((3,)),
        s_3=DMA((7,)), r_3=DMA((7,)),
        s_4=DMA((7,)), r_4=DMA((7,)),
        s_5=DMA((11,)), r_5=DMA((11,)),
        s_a=DMA((2, 18)), r_a=DMA((2, 18)),
    )
    for k in range(2):
        for n, name in ((2, "c"), (4, "x"), (4, "y"), (8, "z")):
            sets["b%d%s" % (k, name)] = VM((n, 2, LANES), F32)
    return sets


class Refs:
    pass


def mega_body(*refs):
    r = Refs()
    names = list(IN_NAMES) + list(OUT_NAMES) + list(scratch_list())
    for name, ref in zip(names, refs, strict=True):
        setattr(r, name, ref)
    x, y, z, c = place()
    u = x * (1 - c) + y * c
    v = y * (1 - c) + x * c
    zl = z % 2
    oz = 1 - zl
    sib = device(x, y, z, 1 - c)

    def at_u(k):
        return device(k * (1 - c) + x * c, y * (1 - c) + k * c, z, c)

    def at_v(k):
        return device(x * (1 - c) + k * c, k * (1 - c) + y * c, z, c)

    others = [sib]
    others += [device((x + k) % 4, y, z, c) for k in range(1, 4)]
    others += [device((x + k) % 4, y, z, 1 - c) for k in range(1, 4)]
    others += [device(x, (y + k) % 4, z, c) for k in range(1, 4)]
    others += [device(x, y, (z + k) % 8, c) for k in range(1, 8)]
    barrier = pltpu.get_barrier_semaphore()
    for d in others:
        pl.semaphore_signal(barrier, inc=1, device_id=d, device_id_type=MESH)
    in_x = pltpu.make_async_copy(r.x_hbm, r.raw, r.s_in.at[0])
    in_x.start()
    in_up = pltpu.make_async_copy(r.up_hbm, r.raw2, r.s_in.at[1])
    in_up.start()
    for s in range(4):
        t = r.tile[s]
        w = dot(t, r.cs[...]).astype(BF)
        we = dot(t, r.cse[...]).astype(BF)
        wee = dot(t, r.csee[...]).astype(BF)
        full = dot(r.rs[...], w) + dot(we, r.rsm[...], ((0,), (0,))) + dot(r.rse[...], wee)
        r.pay[s] = full.astype(BF)
    pl.semaphore_wait(barrier, len(others))
    sends = []

    acc = r.acc

    def first_x():
        in_x.wait()
        load_native(r.raw, r.xn)
        zero_borders(r.xb)
        acc[...] = jnp.zeros_like(acc)

    def permute(lo, hi, sink):
        def step(g, carry):
            p = dot(r.xn[:, :, lanes_of(g, 2)].reshape(ROWS, 256), r.pg[g])
            sink(g, p[:, :128])
            acc[...] += p[:, 128:]
            return carry

        lax.fori_loop(lo, hi, step, 0)

    def keep_x(g, val):
        store_shifts(r.xb, val, lanes_of(g))

    def keep_up(g, val):
        r.upp[:, lanes_of(g)] = val.astype(BF)

    def last_x():
        keep_x(GROUPS, acc[...])
        r.ex[...] = dot(tap_concat(r.xb, lanes_of(12), False), r.ry[...]).astype(BF)

    def first_up():
        in_up.wait()
        load_native(r.raw2, r.xn)
        zero_borders(r.ghb)
        acc[...] = jnp.zeros_like(acc)

    thunks = [first_x]
    thunks += [lambda k=k: permute(3 * k, 3 * k + 3, keep_x) for k in range(4)]
    thunks += [last_x, first_up]
    thunks += [lambda k=k: permute(3 * k, 3 * k + 3, keep_up) for k in range(4)]
    thunks += [lambda: keep_up(GROUPS, acc[...])]

    def work():
        if thunks:
            thunks.pop(0)()

    gat = r.gat

    def chunk(i, j, zz):
        lin = c * 128 + ((v + i) % 4) * 32 + ((u + j) % 4) * 8 + zz * 4
        return lambda h=None: gat.at[pl.ds(lin, 4)] if h is None else gat.at[pl.ds(lin + 2 * h, 2)]

    mine = c * 128 + v * 32 + u * 8 + zl * 4 + c * 2
    other = (1 - c) * 128 + u * 32 + v * 8 + zl * 4 + c * 2
    gat[pl.ds(mine, 2)] = r.pay[pl.ds(2 * c, 2)]
    gat[pl.ds(other, 2)] = r.pay[pl.ds(2 - 2 * c, 2)]
    mine, other = gat.at[pl.ds(mine, 2)], gat.at[pl.ds(other, 2)]
    sib_copy = send(other, other, r.s_sib.at[0], r.r_sib.at[0], sib)
    own_copy = send(mine, mine, r.s_d.at[32], r.r_d.at[32], sib)
    sends += [sib_copy, own_copy]
    sib_copy.wait_recv()

    k = chunk(0, 0, zl)
    z0 = send(k(0), k(0), r.s_z.at[0], r.r_z.at[0], device(x, y, (z + 1) % 8, c))
    z1 = send(k(1), k(1), r.s_z.at[1], r.r_z.at[1], device(x, y, (z + 7) % 8, c))
    sends += [z0, z1]

    def spread(n, k, ss, rs, at, p):
        pair = [send(k(), k(), ss.at[n, 0], rs.at[n, 0], at((p + 1) % 4)),
                send(k(), k(), ss.at[n, 1], rs.at[n, 1], at((p + 3) % 4))]
        sends.extend(pair)
        return pair

    def spread_u(n, zz):
        return spread(n, chunk(0, 0, zz), r.s_u, r.r_u, at_u, u)

    def spread_v(n, k):
        return spread(n, k, r.s_v, r.r_v, at_v, v)

    def pass_on(n, k):
        sends.append(send(k(), k(), r.s_d.at[n], r.r_d.at[n], sib))

    order = [(0, zl), (0, oz), (3, zl), (1, zl), (3, oz), (1, oz), (2, zl), (2, oz)]
    ring_u, ring_v = {}, {}
    ring_u[0] = spread_u(0, zl)
    ring_v[0] = spread_v(0, chunk(0, 0, zl))
    work()
    z0.wait_recv()
    z1.wait_recv()
    ring_u[1] = spread_u(1, oz)
    ring_v[1] = spread_v(1, chunk(0, 0, oz))
    pass_on(1, chunk(0, 0, oz))
    half_u = {}
    for n, zz in ((0, zl), (1, oz)):
        work()
        ring_u[n][0].wait_recv()
        k = chunk(0, 3, zz)
        h0 = send(k(0), k(0), r.s_u.at[n, 2], r.r_u.at[n, 2], at_u((u + 1) % 4))
        ring_v[2 + 2 * n] = spread_v(2 + 2 * n, k)
        pass_on(2 + 2 * n, k)
        ring_u[n][1].wait_recv()
        k = chunk(0, 1, zz)
        h1 = send(k(1), k(1), r.s_u.at[n, 3], r.r_u.at[n, 3], at_u((u + 3) % 4))
        ring_v[3 + 2 * n] = spread_v(3 + 2 * n, k)
        pass_on(3 + 2 * n, k)
        sends += [h0, h1]
        half_u[n] = (h0, h1)
    for n, zz in ((0, zl), (1, oz)):
        work()
        half_u[n][0].wait_recv()
        half_u[n][1].wait_recv()
        k = chunk(0, 2, zz)
        ring_v[6 + n] = spread_v(6 + n, k)
        pass_on(6 + n, k)
    half_v = {}
    for n, (j, zz) in enumerate(order):
        work()
        ring_v[n][0].wait_recv()
        k = chunk(3, j, zz)
        h0 = send(k(0), k(0), r.s_v.at[n, 2], r.r_v.at[n, 2], at_v((v + 1) % 4))
        pass_on(8 + n, k)
        ring_v[n][1].wait_recv()
        k = chunk(1, j, zz)
        h1 = send(k(1), k(1), r.s_v.at[n, 3], r.r_v.at[n, 3], at_v((v + 3) % 4))
        pass_on(16 + n, k)
        sends += [h0, h1]
        half_v[n] = (h0, h1)
    for n, (j, zz) in enumerate(order):
        half_v[n][0].wait_recv()
        half_v[n][1].wait_recv()
        pass_on(24 + n, chunk(2, j, zz))
    while thunks:
        work()
    for n in range(1, 32):
        k = gat.at[pl.ds((1 - c) * 128, 4)]
        pltpu.make_async_remote_copy(
            src_ref=k, dst_ref=k, send_sem=r.s_d.at[n], recv_sem=r.r_d.at[n],
            device_id=sib, device_id_type=MESH,
        ).wait_recv()
    own_copy.wait_recv()
    for copy in sends:
        copy.wait_send()
    sends = []

    def pull(t, carry):
        g, q = t // 12, t % 12
        s = r.idx[t]
        r.bm[g, pl.ds(pl.multiple_of(q * 96, 32), 96), :] = gat[s, 0:96, :]
        r.ta[g, q] = gat[s, 96:112, :]
        return carry

    lax.fori_loop(0, 144, pull, 0)
    for q in range(12):
        m = dot(r.ta[:, q].reshape(192, 128), r.selm[...], ((0,), (0,)))
        r.me[96 * q : 96 * q + 96, :] = m[0:96].astype(BF)
    acc[...] = jnp.zeros_like(acc)
    valid = (lax.broadcasted_iota(jnp.int32, (ROWS, 128), 0) % 32) < 28

    def stat(h, lanes):
        h = jnp.where(valid, h.astype(F32), 0.0)
        r.lsum[0:1, lanes] = jnp.sum(h, axis=0, keepdims=True)
        r.lsum[1:2, lanes] = jnp.sum(h * h, axis=0, keepdims=True)

    def fstep(yy, carry):
        for gg in range(3):
            g = 3 * yy + gg
            here = (lane_iota(1152) // 4) == yy * 4 + gg
            bg = r.bg
            bg[0:1152, 0:128] = r.bm[g]
            bg[0:1152, 128:256] = jnp.where(here, r.me[...].astype(F32), 0.0).astype(BF)
            tails = r.ta[g].reshape(192, 128)
            bg[1152:1280, 0:128] = dot(r.sele[0, gg], tails).astype(BF)
            ee = jnp.where(here[0:128], dot(r.sele[1, gg], tails), 0.0)
            bg[1152:1280, 128:256] = ee.astype(BF)
            a = tap_concat(r.xb, lanes_of(g), False, r.ex[:, lanes_of(yy)])
            p = dot(a, bg[...])
            h = p[:, :128].astype(BF)
            r.hid[:, lanes_of(g)] = h
            stat(h, lanes_of(g))
            acc[...] += p[:, 128:]
        return carry

    lax.fori_loop(0, 4, fstep, 0)
    h = acc[...].astype(BF)
    r.hid[:, 1536:1664] = h
    stat(h, lanes_of(12))

    def all_sum(k, src, dst, fill):
        value = src[...]
        base = 0
        stages = [
            ("c", 2, c, lambda q: device(x, y, z, q)),
            ("x", 4, x, lambda q: device(q, y, z, c)),
            ("y", 4, y, lambda q: device(x, q, z, c)),
            ("z", 8, z, lambda q: device(x, y, q, c)),
        ]
        for name, n, p, dev in stages:
            buf = getattr(r, "b%d%s" % (k, name))
            buf[p] = value
            copies = [
                send(buf.at[p], buf.at[p], r.s_a.at[k, base + i], r.r_a.at[k, base + i], dev((p + i) % n))
                for i in range(1, n)
            ]
            sends.extend(copies)
            if fill:
                fill.pop(0)()
            for copy in copies:
                copy.wait_recv()
            value = buf[0]
            for i in range(1, n):
                value = value + buf[i]
            base += n
        dst[...] = value

    def make_tr():
        tr_in = jnp.concatenate([r.me[128 * tap : 128 * tap + 128] for tap in range(9)], axis=1)
        r.tr[...] = dot(tr_in, r.ry[...]).astype(BF)
        r.wt[128:256, :] = jnp.zeros((128, 1280), BF)

    all_sum(0, r.lsum, r.sums, [make_tr])

    def tile(t, carry):
        lanes = lanes_of(t)
        avg = r.sums[0:1, lanes] / TOTAL
        inv = lax.rsqrt(r.sums[1:2, lanes] / TOTAL - avg * avg + EPSILON)
        gain, bias = r.par[0:1, lanes], r.par[1:2, lanes]
        s1 = jnp.zeros((8, 128), F32)
        s2 = jnp.zeros((8, 128), F32)
        for k in range(28):
            rows = pl.ds(16 * k, 16)
            xv = r.xb[1, 1 + k // 2, 16 * (k % 2) : 16 * (k % 2) + 16, lanes].astype(F32)
            normed = (r.hid[rows, lanes].astype(F32) - avg) * inv
            aff = gain * normed + bias
            sa = half_tanh(aff)
            act = aff * sa
            summed = xv + act
            ss = half_tanh(summed)
            out = summed * ss
            r.bo[rows, lanes] = out.astype(BF)
            gsv = r.upp[rows, lanes].astype(F32) * (ss + out * (1.0 - ss))
            gav = gsv * (sa + act * (1.0 - sa))
            r.gs[rows, lanes] = gsv
            r.ga[rows, lanes] = gav
            p = gav * normed
            s1 = s1 + (p[0:8] + p[8:16])
            s2 = s2 + (gav[0:8] + gav[8:16])
        r.lsum[0:1, lanes] = jnp.sum(s1, axis=0, keepdims=True)
        r.lsum[1:2, lanes] = jnp.sum(s2, axis=0, keepdims=True)
        return carry

    lax.fori_loop(0, 13, tile, 0)

    def unpermute(lo, hi, src):
        def step(g, carry):
            pair = jnp.concatenate([src(g), src(GROUPS)], axis=1)
            p = dot(pair, r.pg[g], ((1,), (1,)))
            r.xn[:, :, lanes_of(g)] = (acc[...] + p[:, :128]).astype(BF).reshape(14, 32, 128)
            acc[...] = p[:, 128:]
            return carry

        if lo == 0:
            acc[...] = jnp.zeros_like(acc)
        lax.fori_loop(lo, hi, step, 0)

    def write_out(raw, hbm, n):
        r.xn[:, :, 1536:1664] = acc[...].astype(BF).reshape(14, 32, 128)
        for yy in range(14):
            raw[yy] = r.xn[yy, 0:28, 0:1584].reshape(14, 2, 1584)
        copy = pltpu.make_async_copy(raw, hbm, r.s_out.at[n])
        copy.start()
        return copy

    outs = []
    from_bo = lambda g: r.bo[:, lanes_of(g)]
    all_sum(1, r.lsum, r.gsum, [
        lambda: unpermute(0, 4, from_bo),
        lambda: unpermute(4, 8, from_bo),
        lambda: unpermute(8, 12, from_bo),
        lambda: outs.append(write_out(r.raw, r.out_hbm, 0)),
    ])

    def gtile(t, carry):
        lanes = lanes_of(t)
        avg = r.sums[0:1, lanes] / TOTAL
        inv = lax.rsqrt(r.sums[1:2, lanes] / TOTAL - avg * avg + EPSILON)
        scale = r.par[0:1, lanes] * inv
        c1 = r.gsum[1:2, lanes] / TOTAL
        c2 = r.gsum[0:1, lanes] / TOTAL
        normed = (r.hid[:, lanes].astype(F32) - avg) * inv
        gh = scale * (r.ga[:, lanes] - c1 - normed * c2)
        store_shifts(r.ghb, jnp.where(valid, gh, 0.0), lanes)
        return carry

    lax.fori_loop(0, 13, gtile, 0)
    r.eg[...] = dot(tap_concat(r.ghb, lanes_of(12), True), r.ry[...]).astype(BF)
    g12 = r.ghb[1, 1:15, :, 1536:1664].reshape(ROWS, 128)
    r.g12t[...] = g12.astype(F32).T.astype(BF)

    st, r0 = r.st, r.r0

    def place_of(k, i, half):
        yy, xx = (y + 1 + k) % 4, (x + 1 + i) % 4
        return yy * (1 - half) + xx * half, xx * (1 - half) + yy * half

    def core_copy(k, i):
        pv, pu = place_of(k, i, 1 - c)
        return pltpu.make_async_remote_copy(
            src_ref=st.at[1 - c, pv, pu], dst_ref=r0.at[pv, pu],
            send_sem=r.s_c.at[4 * k + i], recv_sem=r.r_c.at[4 * k + i],
            device_id=sib, device_id_type=MESH,
        )

    def v_copy(rel, ju):
        q = (v + 1 + rel) % 4
        return pltpu.make_async_remote_copy(
            src_ref=r0.at[q, (u + 1 + ju) % 4], dst_ref=r.r1.at[rel, ju],
            send_sem=r.s_1.at[4 * rel + ju], recv_sem=r.r_1.at[4 * rel + ju],
            device_id=at_v(q), device_id_type=MESH,
        )

    def add_core(k):
        for i in range(4):
            core_copy(k, i).wait_recv()
            pv, pu = place_of(k, i, c)

            def add(n, carry):
                row = pl.ds(pl.multiple_of(n * 128, 128), 128)
                total = st[c, pv, pu, row, :].astype(F32) + r0[pv, pu, row, :].astype(F32)
                r0[pv, pu, row, :] = total.astype(BF)
                return carry

            lax.fori_loop(0, 4, add, 0)
            if i < 3:
                @pl.when(c == 1)
                def _():
                    v_copy(i, k).start()

            @pl.when((c == 0) & (k < 3))
            def _():
                v_copy(k, i).start()

    def wstep(k, carry):
        yy = (y + 1 + k) % 4
        acc[0:144, :] = jnp.zeros((144, 128), F32)
        r.mec[...] = jnp.zeros_like(r.mec)
        lhs12 = r.g12t[rows_at(16 * yy, 16), :]
        for gg in range(3):
            g = 3 * yy + gg
            main = r.ghb[1, 1:15, :, lanes_of(g)].reshape(ROWS, 128)
            lhs = jnp.concatenate([main.astype(F32).T.astype(BF), lhs12], axis=0)
            a = tap_concat(r.xb, lanes_of(g), False, r.ex[:, lanes_of(yy)])
            p = dot(lhs, a)
            for tap in range(9):
                px, pos = piece_of(gg * 9 + tap)
                blk = p[0:128, tap * 128 : tap * 128 + 128].astype(BF)
                st[0, yy, px, pos * 64 : pos * 64 + 64, :] = blk[0:64]
                st[1, px, yy, pos * 64 : pos * 64 + 64, :] = blk[64:128]
            rowsel = (lax.broadcasted_iota(jnp.int32, (16, 1152), 0) // 4) == gg
            r.mec[...] += jnp.where(rowsel, p[128:144, 0:1152], 0.0)
            lane = lane_iota(144)
            lanesel = (lane >= 36 * gg) & (lane < 36 * gg + 36)
            row = lax.broadcasted_iota(jnp.int32, (144, 128), 0)
            rowsel = (row < 128) | (row // 4 == 32 + gg)
            acc[0:144, :] += jnp.where(lanesel & rowsel, p[:, 1152:1280], 0.0)
        zeros = jnp.zeros((128, 128), BF)
        for px in range(3):
            for j in range(3):
                tap = 3 * px + j
                st[0, yy, px, 448 + 16 * j : 464 + 16 * j, :] = r.mec[:, 128 * tap : 128 * tap + 128].astype(BF)
            st[1, px, yy, 448:496, :] = acc[48 * px : 48 * px + 48, :].astype(BF)
            st[0, yy, px, 496:512, :] = zeros[0:16]
            st[1, px, yy, 496:512, :] = zeros[0:16]
        st[0, yy, 3, 384:512, :] = zeros
        st[1, 3, yy, 384:512, :] = zeros
        for i in range(4):
            core_copy(k, i).start()

        @pl.when(k > 0)
        def _():
            add_core(k - 1)

        return carry

    lax.fori_loop(0, 4, wstep, 0)

    def back_set(yy):
        block = pl.ds(128 + 16 * yy, 16)
        wt = r.wt

        def bstep(gg, carry):
            g = 3 * yy + gg
            for tap in range(9):
                wt[0:128, 128 * tap : 128 * tap + 128] = r.bm[g, 128 * tap : 128 * tap + 128, :]
            lane = lane_iota(128)
            lanesel = (lane >= 36 * gg) & (lane < 36 * gg + 36)
            wt[0:128, 1152:1280] = jnp.where(lanesel, r.tr[:, lanes_of(yy)].astype(F32), 0.0).astype(BF)
            tails = r.ta[g].reshape(192, 128)
            bl = dot(r.selb[0, gg], tails).astype(BF)
            be = dot(r.selb[1, gg], tails)
            low = jnp.zeros((16, 128), F32)
            lane = lane_iota(16)
            for tap in range(9):
                wt[block, 128 * tap : 128 * tap + 128] = bl[16 * tap : 16 * tap + 16]
                low = jnp.where((lane // 4) == 9 * gg + tap, be[16 * tap : 16 * tap + 16], low)
            wt[block, 1152:1280] = low.astype(BF)
            a = tap_concat(r.ghb, lanes_of(g), True, r.eg[:, lanes_of(yy)])
            p = dot(a, wt[...], ((1,), (1,)))
            r.gs[:, lanes_of(g)] += p[:, :128]
            r.gs[:, 1536:1664] += p[:, 128:]
            return carry

        lax.fori_loop(0, 3, bstep, 0)
        wt[block, :] = jnp.zeros((16, 1280), BF)

    def sum_v(ju):
        for rel in range(3):
            v_copy(rel, ju).wait_recv()
        pu = (u + 1 + ju) % 4

        def add(n, carry):
            row = pl.ds(pl.multiple_of(n * 128, 128), 128)
            total = r0[v, pu, row, :].astype(F32)
            for rel in range(3):
                total = total + r.r1[rel, ju, row, :].astype(F32)
            r.cur2[ju, row, :] = total.astype(BF)
            return carry

        lax.fori_loop(0, 4, add, 0)
        if ju < 3:
            send_u = send(r.cur2.at[ju], r.r2.at[ju], r.s_2.at[ju], r.r_2.at[ju], at_u(pu))
            u_copies.append(send_u)

    u_copies = []
    back_set(0)
    add_core(3)
    back_set(1)
    back_set(2)
    sum_v(0)
    sum_v(1)
    back_set(3)
    sum_v(2)
    sum_v(3)
    from_gs = lambda g: r.gs[:, lanes_of(g)].astype(BF)
    unpermute(0, 4, from_gs)
    for copy in u_copies:
        copy.wait_recv()
    sends += u_copies
    for n in range(8):
        row = pl.ds(64 * n, 64)
        total = r.cur2[3, row, :].astype(F32)
        for rel in range(3):
            total = total + r.r2[rel, row, :].astype(F32)
        r.cur3[n] = total.astype(BF)
    copies = []
    for k in range(1, 8):
        q = (z + k) % 8
        copies.append(send(r.cur3.at[q], r.r3.at[k - 1], r.s_3.at[k - 1], r.r_3.at[k - 1], device(x, y, q, c)))
    sends += copies
    unpermute(4, 8, from_gs)
    for copy in copies:
        copy.wait_recv()
    total = r.cur3[z].astype(F32)
    for k in range(7):
        total = total + r.r3[k].astype(F32)
    hh = r.hh
    hh[c, x, z] = total.astype(BF)
    here = hh.at[c, x, z]
    copies = []
    for k in range(1, 8):
        q = (z + k) % 8
        copies.append(send(here, here, r.s_4.at[k - 1], r.r_4.at[k - 1], device(x, y, q, c)))
    sends += copies
    unpermute(8, 12, from_gs)
    outs.append(write_out(r.raw2, r.ig_hbm, 1))
    for copy in copies:
        copy.wait_recv()
    near = [(1, 6 - 3 * (x % 2) - 3 * (x // 3)), (3, 3 - 3 * (x % 2))]
    copies = [send(hh.at[c, x], hh.at[c, x], r.s_5.at[0], r.r_5.at[0], sib)]
    n = 1
    for cc in (c, 1 - c):
        for rel, pos in near:
            to = device((x + rel) % 4, y, z, cc)
            copies.append(send(hh.at[c, x, pos], hh.at[c, x, pos], r.s_5.at[n], r.r_5.at[n], to))
            copies.append(send(hh.at[c, x, 7], hh.at[c, x, 7], r.s_5.at[n + 1], r.r_5.at[n + 1], to))
            n += 2
        to = device((x + 2) % 4, y, z, cc)
        copies.append(send(hh.at[c, x, 7], hh.at[c, x, 7], r.s_5.at[n], r.r_5.at[n], to))
        n += 1
    for copy in copies:
        copy.wait_recv()
    sends += copies
    sp = (z % 2) * 8 + x * 2 + c
    b0 = (sp * 29403) // 17424 - sp // 15
    em = jnp.concatenate([hh[1, j, 7, 0:48, :] for j in range(3)], axis=0)
    for k in range(3):
        b = b0 + k
        px, pos = piece_of(b)
        tap = b % 9
        gg = b // 9
        main = jnp.concatenate([hh[0, px, pos], hh[1, px, pos]], axis=0)
        mrow = hh[0, tap // 3, 7, rows_at(16 * (tap % 3), 16), :]
        left = jnp.concatenate([main, mrow], axis=0)
        line = lax.broadcasted_iota(jnp.int32, (128, 136), 0) - (36 * gg + 4 * tap)
        unit = lax.broadcasted_iota(jnp.int32, (128, 136), 1)
        qe = jnp.where((line >= 0) & (line < 4) & (unit == 33 * line + 32), 1.0, 0.0).astype(BF)
        t1 = (dot(left, r.qm[...]) + dot(em, qe)).astype(BF)
        t2 = dot(t1, r.qo[gg], ((0,), (0,)))
        r.kg[pl.ds(132 * k, 132), :] = t2[0:132]

    for copy in sends:
        copy.wait_send()
    for k in range(4):
        for i in range(4):
            core_copy(k, i).wait_send()
    for rel in range(3):
        for ju in range(4):
            v_copy(rel, ju).wait_send()
    for copy in outs:
        copy.wait()


def mega(idx, tiles, par, xt, upt):
    k = constants()
    operands = [idx, tiles, *prep_constants(), par, k["pg"], k["ry"], k["selm"], k["sele"], k["selb"], *fin_constants(), xt, upt]
    anywhere = pl.BlockSpec(memory_space=pl.ANY)
    return pl.pallas_call(
        mega_body,
        in_specs=[pl.BlockSpec(memory_space=pltpu.SMEM)] + [vspec()] * 15 + [anywhere] * 2,
        out_specs=[anywhere, anywhere, vspec(), vspec()],
        out_shape=[
            struct((14, 14, 2, 1584), BF),
            struct((14, 14, 2, 1584), BF),
            struct((396, GW), F32),
            struct((2, LANES), F32),
        ],
        scratch_shapes=list(scratch_list().values()),
        compiler_params=pltpu.CompilerParams(
            collective_id=1, has_side_effects=True, vmem_limit_bytes=VLIM
        ),
        name="block",
    )(*operands)


def channels_in(v):
    p = v.reshape(4, 3, 4, 33)
    main = p[..., :32].reshape(1536)
    extra = jnp.pad(p[..., 32].reshape(4, 12), ((0, 0), (0, 4))).reshape(64)
    return jnp.concatenate([main, extra, jnp.zeros((64,), v.dtype)])


def channels_out(v):
    main = v[:1536].reshape(4, 3, 4, 32)
    extra = v[1536:1600].reshape(4, 16)[:, :12].reshape(4, 3, 4, 1)
    return jnp.concatenate([main, extra], axis=-1).reshape(1584)


def tile_rows(tile_counts, owner_order):
    run_end = jnp.cumsum(tile_counts)
    run_start = run_end - tile_counts
    tile_ids = jnp.arange(144, dtype=jnp.int32)
    rank_of = jnp.sum((run_end[None, :] <= tile_ids[:, None]).astype(jnp.int32), axis=1)
    onehot = (rank_of[:, None] == jnp.arange(64, dtype=jnp.int32)[None, :]).astype(jnp.int32)
    s = jnp.sum(onehot * owner_order[None, :], axis=1)
    j = tile_ids - jnp.sum(onehot * run_start[None, :], axis=1)
    y, zl, x, core = s // 16, (s // 8) % 2, (s // 2) % 4, s % 2
    vu = jnp.where(j < 2, y * 4 + x, x * 4 + y)
    return (j // 2) * 128 + vu * 8 + zl * 4 + core * 2 + j % 2


def local(block_input, upstream, kernel_tiles, tile_counts, owner_order, gain, bias):
    idx = tile_rows(tile_counts, owner_order)
    par = jnp.stack([channels_in(gain), channels_in(bias)])
    turn = lambda a: jnp.transpose(a, (1, 2, 0, 3))
    back = lambda a: jnp.transpose(a, (2, 0, 1, 3))
    out, ig, kg, gsum = mega(
        idx, kernel_tiles.reshape(4, 99, GW), par, turn(block_input), turn(upstream)
    )
    sp = lax.axis_index("shard") % 16
    b0 = (sp * 29403) // 17424 - sp // 15
    kernel_grad = lax.dynamic_slice(kg.reshape(-1), (sp * 29403 - b0 * 17424,), (29403,))
    return (back(out), back(ig), kernel_grad, channels_out(gsum[0]), channels_out(gsum[1]))


def solution(mesh):
    return jax.shard_map(
        local,
        mesh=mesh,
        in_specs=(
            P(("dp", "shard"), None, None, None),
            P(("dp", "shard"), None, None, None),
            P("shard", None),
            P(),
            P(),
            P(),
            P(),
        ),
        out_specs=(
            P(("dp", "shard"), None, None, None),
            P(("dp", "shard"), None, None, None),
            P("shard"),
            P(),
            P(),
        ),
        check_vma=False,
    )
```

time: 980 us -> 138 us (0.14); the launches traced: 961 us -> 138 us
  blocking collectives: 487 us -> 0 us
  local copies, waits for them, and re-layouts: 410 us -> 15.3 us
  Pallas kernels: 0 us -> 118 us
  matrix products: 34.7 us -> 0 us
  between operations: 15.3 us -> 0.75 us
  other arithmetic: 13.6 us -> 3.1 us
    unnamed x1 -> x0, blocking collectives: 318 us -> none
    another operation x39 -> x6, local copies, waits for them, and re-layouts: 255 us -> 0.92 us  [the longest x38 255 us: tap_columns(): return jnp.stack(pieces, axis=2)]
    psum x3 -> x0, blocking collectives: 169 us -> none  [the longest x1 81.6 us: local(): lax.psum((jnp.sum(values, axis=(0, 1, 2)), jnp.sum(values * values, axis=...]
    pallas_call x0 -> x1, Pallas kernels: none -> 118 us  [mega(): pl.pallas_call(mega_body, in_specs=[pl.BlockSpec(memory_space=pltpu.SMEM)...]
    unnamed x74 -> x4, local copies, waits for them, and re-layouts: 44.3 us -> 4.42 us
    reshape x4 -> x16, local copies, waits for them, and re-layouts: 46.6 us -> 7.14 us  [the longest x1 1.89 us: local(): kernel_tiles.reshape(4, 99, GW)]
    dot_general x3 -> x0, matrix products: 34.7 us -> none  [the longest x1 13.3 us: local(): jnp.einsum('rgti,rgo->gtio', input_columns, grad_rows, preferred_element_...]
    slice x10 -> x4, local copies, waits for them, and re-layouts: 31.1 us -> 1.93 us  [the longest x1 0.82 us: channels_out(): main = v[:1536].reshape(4, 3, 4, 32)]
  transfers between devices with their start and end apart: 1 -> 0, of which waited for: 0 -> 0; matrix products, arithmetic and copies ran while one was open for 18% -> 0% of each run, Pallas kernels for 0% -> 0%
where the time goes in v2:
time: 138 us
  Pallas kernels  118 us (86%)
  local copies, waits for them, and re-layouts  15.3 us (11%)
  other arithmetic  3.1 us (2%)
    pallas_call x1, Pallas kernels, mega(): pl.pallas_call(mega_body, in_specs=[pl.BlockSpec(memory_space=pltpu.SMEM)...  118 us
    unnamed x4, local copies, waits for them, and re-layouts  4.42 us

profile of v2, /device:TPU:1, one launch (start us, length us, event | category | flops | bytes accessed | tf_op | source)
XLA Modules:
  0.0 137.7 jit_solution(12110374406178426588)
XLA Ops:
  0.7 0.8 reshape.98
  1.5 0.2 slice_reduce_fusion
  1.7 0.1 reshape_squeeze.7
  1.8 0.1 reshape.100
  1.9 0.1 reshape.99
  2.0 0.1 concatenate.13
  2.0 0.8 reshape.95
  2.9 0.2 slice_reduce_fusion.1
  3.1 0.1 reshape_squeeze.6
  3.1 0.1 reshape.97
  3.2 0.1 reshape.96
  3.3 0.1 concatenate.12
  3.4 0.6 pad_maximum_fusion.2.refs_8_
  4.0 0.7 copy.31
  4.8 0.1 reduce-window.8
  4.9 0.1 reduce
  5.0 0.1 convert_reduce_fusion
  5.1 0.7 sub.37
  5.7 0.7 select_reduce_fusion.1
  6.5 0.6 fusion.4.refs_0_
  7.1 1.9 %reshape.94.refs_1_ = bf16[4,99,132]{2,1,0:T(8,128)(2,1)} reshape(bf16[4,13068]{1,0:T(4,128)(2,1)} %param.22) | data formatting | bytes 209088 | tf_op jit(solution)/shard_map/reshape | solution.py:866
  9.0 118.5 %block.1 = (bf16[14,14,2,1584]{3,2,1,0:T(2,128)(2,1)}, bf16[14,14,2,1584]{3,2,1,0:T(2,128)(2,1)}, f32[396,132]{1,0:T(8,128)}, f32[2,1664]{1,0:T(2,128)}) custom-call(s32[144]{0:T(256)} %fusion.4.refs_0_, bf16[4,99,132]{2,1,0:T(8,128)(2,1)} %reshape.94.refs_1_, bf16[132,128]{1,0:T(8,128)(2,1)} %constant.151.clone.refs_2_, ...), custom_call_target="tpu_custom_call" | custom-call | tf_op jit(solution)/shard_map/block/pallas_call | solution.py:816
  127.5 1.3 reshape.101
  128.7 0.8 dynamic_slice.3
  129.5 0.8 slice_reduce_fusion.2
  130.3 0.1 reshape.106
  130.4 0.8 slice_reduce_fusion.4
  131.2 0.1 reshape.107
  131.3 0.1 reshape.111
  131.4 0.1 pad_maximum_fusion.1
  131.4 0.7 reshape.109
  132.2 0.1 reshape.102
  132.3 0.1 reshape.103
  132.3 0.1 reshape.110
  132.4 0.1 pad_maximum_fusion
  132.5 0.7 reshape.105
  133.3 0.0 copy-start
  133.3 3.4 %copy.36 = bf16[2,14,14,1584]{3,0,2,1:T(2,128)(2,1)} copy(bf16[2,14,14,1584]{3,0,2,1:T(2,128)(2,1)} %bitcast.12) | data formatting | bytes 2483712
  136.6 0.0 copy-done
  136.6 1.1 copy.37
  (5 shorter events, 0.0 us)
Async XLA Ops:
  133.3 3.4 %copy-start = (bf16[14,14,2,1584]{3,2,1,0:T(2,128)(2,1)S(1)}, bf16[14,14,2,1584]{3,2,1,0:T(2,128)(2,1)}, u32[]{:S(2)}) copy-start(bf16[14,14,2,1584]{3,2,1,0:T(2,128)(2,1)} %get-tuple-element.10) | copy-start | bytes 3725572

commit v3 on v2

--- a/solution.py
+++ b/solution.py
@@ -185,10 +185,11 @@
 
 
 IN_NAMES = (
-    "idx", "tile", "cs", "cse", "csee", "rs", "rsm", "rse", "par",
-    "pg", "ry", "selm", "sele", "selb", "qm", "qo", "x_hbm", "up_hbm",
+    "idx", "tile", "cs", "cse", "csee", "rs", "rsm", "rse", "gain", "bias",
+    "pg_h", "ry_h", "selm_h", "sele_h", "selb_h", "qm_h", "qo_h", "x_hbm", "up_hbm",
 )
-OUT_NAMES = ("out_hbm", "ig_hbm", "kg", "gsum")
+LOADED = ("pg", "ry", "selm", "sele", "selb", "qm", "qo")
+OUT_NAMES = ("out_hbm", "ig_hbm", "kg", "gg_out", "bg_out")
 
 
 def scratch_list():
@@ -210,7 +211,7 @@
         raw=VM((14, 14, 2, 1584), BF),
         raw2=VM((14, 14, 2, 1584), BF),
         xn=VM((14, 32, LANES), BF),
-        acc=VM((ROWS, 128), F32),
+        acc=VM((ROWS + 16, 128), F32),
         mec=VM((16, 1152), F32),
         bg=VM((1280, 256), BF),
         wt=VM((256, 1280), BF),
@@ -218,32 +219,48 @@
         g12t=VM((128, ROWS), BF),
         st=VM((2, 4, 4, 512, 128), BF),
         r0=VM((4, 4, 512, 128), BF),
-        r1=VM((3, 4, 512, 128), BF),
+        ra=VM((4, 256, 128), BF),
+        rb=VM((4, 256, 128), BF),
+        rp=VM((4, 512, 128), BF),
+        rm=VM((4, 512, 128), BF),
         cur2=VM((4, 512, 128), BF),
         r2=VM((3, 512, 128), BF),
         cur3=VM((8, 64, 128), BF),
         r3=VM((7, 64, 128), BF),
         hh=VM((2, 4, 8, 64, 128), BF),
-        sums=VM((2, LANES), F32),
-        lsum=VM((2, LANES), F32),
+        sums=VM((2, 16, 128), F32),
+        gsum=VM((2, 16, 128), F32),
+        lsum=VM((2, 16, 128), F32),
+        par=VM((2, 16, 128), F32),
+        pf=VM((16, LANES), F32),
+        pn=VM((16, LANES), BF),
+        og=VM((2, LANES), F32),
+        pg=VM((GROUPS, 256, 256), BF),
+        ry=VM((1152, 512), BF),
+        selm=VM((192, 128), BF),
+        sele=VM((2, 3, 128, 192), BF),
+        selb=VM((2, 3, 144, 192), BF),
+        qm=VM((128, 136), BF),
+        qo=VM((3, 144, GW), BF),
         s_in=DMA((2,)),
+        s_k=DMA((7,)),
         s_out=DMA((2,)),
         s_sib=DMA((1,)), r_sib=DMA((1,)),
-        s_z=DMA((2,)), r_z=DMA((2,)),
+        s_z=DMA((11, 2)), r_z=DMA((11, 2)),
         s_u=DMA((2, 4)), r_u=DMA((2, 4)),
         s_v=DMA((8, 4)), r_v=DMA((8, 4)),
         s_d=DMA((33,)), r_d=DMA((33,)),
         s_c=DMA((16,)), r_c=DMA((16,)),
-        s_1=DMA((12,)), r_1=DMA((12,)),
+        s_1=DMA((6, 4)), r_1=DMA((6, 4)),
         s_2=DMA((3,)), r_2=DMA((3,)),
         s_3=DMA((7,)), r_3=DMA((7,)),
         s_4=DMA((7,)), r_4=DMA((7,)),
         s_5=DMA((11,)), r_5=DMA((11,)),
-        s_a=DMA((2, 18)), r_a=DMA((2, 18)),
+        s_a=DMA((2, 25)), r_a=DMA((2, 25)),
+        buf_c=VM((2, 16, 128), F32),
+        buf_p=VM((2, 16, 16, 128), F32),
+        buf_z=VM((2, 8, 16, 128), F32),
     )
-    for k in range(2):
-        for n, name in ((2, "c"), (4, "x"), (4, "y"), (8, "z")):
-            sets["b%d%s" % (k, name)] = VM((n, 2, LANES), F32)
     return sets
 
 
@@ -270,9 +287,8 @@
         return device(x * (1 - c) + k * c, k * (1 - c) + y * c, z, c)
 
     others = [sib]
-    others += [device((x + k) % 4, y, z, c) for k in range(1, 4)]
+    others += [device((x + k % 4) % 4, (y + k // 4) % 4, z, c) for k in range(1, 16)]
     others += [device((x + k) % 4, y, z, 1 - c) for k in range(1, 4)]
-    others += [device(x, (y + k) % 4, z, c) for k in range(1, 4)]
     others += [device(x, y, (z + k) % 8, c) for k in range(1, 8)]
     barrier = pltpu.get_barrier_semaphore()
     for d in others:
@@ -281,6 +297,24 @@
     in_x.start()
     in_up = pltpu.make_async_copy(r.up_hbm, r.raw2, r.s_in.at[1])
     in_up.start()
+    loads = [
+        pltpu.make_async_copy(getattr(r, name + "_h"), getattr(r, name), r.s_k.at[n])
+        for n, name in enumerate(LOADED)
+    ]
+    for load in loads:
+        load.start()
+
+    def split3(val):
+        hi = val.astype(BF).astype(F32)
+        mid = (val - hi).astype(BF).astype(F32)
+        return hi, mid, val - hi - mid
+
+    r.pf[...] = jnp.zeros_like(r.pf)
+    for n, ref in ((0, r.gain), (3, r.bias)):
+        for k, part in enumerate(split3(ref[...].reshape(1, 1584))):
+            r.pf[n + k : n + k + 1, 0:1584] = part
+    r.pn[...] = r.pf[...].astype(BF)
+    r.lsum[...] = jnp.zeros_like(r.lsum)
     for s in range(4):
         t = r.tile[s]
         w = dot(t, r.cs[...]).astype(BF)
@@ -294,6 +328,8 @@
     acc = r.acc
 
     def first_x():
+        for load in loads:
+            load.wait()
         in_x.wait()
         load_native(r.raw, r.xn)
         zero_borders(r.xb)
@@ -301,18 +337,27 @@
 
     def permute(lo, hi, sink):
         def step(g, carry):
-            p = dot(r.xn[:, :, lanes_of(g, 2)].reshape(ROWS, 256), r.pg[g])
+            rows = jnp.concatenate(
+                [r.xn[:, :, lanes_of(g, 2)].reshape(ROWS, 256), r.pn[:, lanes_of(g, 2)]], axis=0
+            )
+            p = dot(rows, r.pg[g])
             sink(g, p[:, :128])
             acc[...] += p[:, 128:]
             return carry
 
         lax.fori_loop(lo, hi, step, 0)
 
+    def row_of(k, t):
+        return (k, pl.ds(t, 1), slice(None))
+
     def keep_x(g, val):
-        store_shifts(r.xb, val, lanes_of(g))
+        store_shifts(r.xb, val[0:ROWS], lanes_of(g))
+        p = val[ROWS:]
+        r.par[row_of(0, g)] = p[0:1] + p[1:2] + p[2:3]
+        r.par[row_of(1, g)] = p[3:4] + p[4:5] + p[5:6]
 
     def keep_up(g, val):
-        r.upp[:, lanes_of(g)] = val.astype(BF)
+        r.upp[:, lanes_of(g)] = val[0:ROWS].astype(BF)
 
     def last_x():
         keep_x(GROUPS, acc[...])
@@ -351,9 +396,13 @@
     sib_copy.wait_recv()
 
     k = chunk(0, 0, zl)
-    z0 = send(k(0), k(0), r.s_z.at[0], r.r_z.at[0], device(x, y, (z + 1) % 8, c))
-    z1 = send(k(1), k(1), r.s_z.at[1], r.r_z.at[1], device(x, y, (z + 7) % 8, c))
-    sends += [z0, z1]
+    def spread_z(m, k):
+        pair = [send(k(0), k(0), r.s_z.at[m, 0], r.r_z.at[m, 0], device(x, y, (z + 1) % 8, c)),
+                send(k(1), k(1), r.s_z.at[m, 1], r.r_z.at[m, 1], device(x, y, (z + 7) % 8, c))]
+        sends.extend(pair)
+        return pair
+
+    z0, z1 = spread_z(0, k)
 
     def spread(n, k, ss, rs, at, p):
         pair = [send(k(), k(), ss.at[n, 0], rs.at[n, 0], at((p + 1) % 4)),
@@ -446,10 +495,10 @@
     acc[...] = jnp.zeros_like(acc)
     valid = (lax.broadcasted_iota(jnp.int32, (ROWS, 128), 0) % 32) < 28
 
-    def stat(h, lanes):
+    def stat(h, t):
         h = jnp.where(valid, h.astype(F32), 0.0)
-        r.lsum[0:1, lanes] = jnp.sum(h, axis=0, keepdims=True)
-        r.lsum[1:2, lanes] = jnp.sum(h * h, axis=0, keepdims=True)
+        r.lsum[row_of(0, t)] = jnp.sum(h, axis=0, keepdims=True)
+        r.lsum[row_of(1, t)] = jnp.sum(h * h, axis=0, keepdims=True)
 
     def fstep(yy, carry):
         for gg in range(3):
@@ -466,27 +515,17 @@
             p = dot(a, bg[...])
             h = p[:, :128].astype(BF)
             r.hid[:, lanes_of(g)] = h
-            stat(h, lanes_of(g))
-            acc[...] += p[:, 128:]
+            stat(h, g)
+            acc[0:ROWS, :] += p[:, 128:]
         return carry
 
     lax.fori_loop(0, 4, fstep, 0)
-    h = acc[...].astype(BF)
+    h = acc[0:ROWS, :].astype(BF)
     r.hid[:, 1536:1664] = h
-    stat(h, lanes_of(12))
+    stat(h, 12)
 
     def all_sum(k, src, dst, fill):
-        value = src[...]
-        base = 0
-        stages = [
-            ("c", 2, c, lambda q: device(x, y, z, q)),
-            ("x", 4, x, lambda q: device(q, y, z, c)),
-            ("y", 4, y, lambda q: device(x, q, z, c)),
-            ("z", 8, z, lambda q: device(x, y, q, c)),
-        ]
-        for name, n, p, dev in stages:
-            buf = getattr(r, "b%d%s" % (k, name))
-            buf[p] = value
+        def share(buf, n, p, base, dev):
             copies = [
                 send(buf.at[p], buf.at[p], r.s_a.at[k, base + i], r.r_a.at[k, base + i], dev((p + i) % n))
                 for i in range(1, n)
@@ -496,11 +535,22 @@
                 fill.pop(0)()
             for copy in copies:
                 copy.wait_recv()
-            value = buf[0]
+            total = buf[0]
             for i in range(1, n):
-                value = value + buf[i]
-            base += n
-        dst[...] = value
+                total = total + buf[i]
+            return total
+
+        half = send(src.at[1 - c], r.buf_c.at[k], r.s_a.at[k, 0], r.r_a.at[k, 0], sib)
+        half.wait_recv()
+        plane, line = r.buf_p.at[k], r.buf_z.at[k]
+        p = y * 4 + x
+        plane[p] = src[c] + r.buf_c[k]
+        line[z] = share(plane, 16, p, 0, lambda q: device(q % 4, q // 4, z, c))
+        dst[c] = share(line, 8, z, 16, lambda q: device(x, y, q, c))
+        rest = send(dst.at[c], dst.at[c], r.s_a.at[k, 24], r.r_a.at[k, 24], sib)
+        rest.wait_recv()
+        half.wait_send()
+        sends.append(rest)
 
     def make_tr():
         tr_in = jnp.concatenate([r.me[128 * tap : 128 * tap + 128] for tap in range(9)], axis=1)
@@ -511,9 +561,9 @@
 
     def tile(t, carry):
         lanes = lanes_of(t)
-        avg = r.sums[0:1, lanes] / TOTAL
-        inv = lax.rsqrt(r.sums[1:2, lanes] / TOTAL - avg * avg + EPSILON)
-        gain, bias = r.par[0:1, lanes], r.par[1:2, lanes]
+        avg = r.sums[row_of(0, t)] / TOTAL
+        inv = lax.rsqrt(r.sums[row_of(1, t)] / TOTAL - avg * avg + EPSILON)
+        gain, bias = r.par[row_of(0, t)], r.par[row_of(1, t)]
         s1 = jnp.zeros((8, 128), F32)
         s2 = jnp.zeros((8, 128), F32)
         for k in range(28):
@@ -534,18 +584,26 @@
             p = gav * normed
             s1 = s1 + (p[0:8] + p[8:16])
             s2 = s2 + (gav[0:8] + gav[8:16])
-        r.lsum[0:1, lanes] = jnp.sum(s1, axis=0, keepdims=True)
-        r.lsum[1:2, lanes] = jnp.sum(s2, axis=0, keepdims=True)
+        r.lsum[row_of(0, t)] = jnp.sum(s1, axis=0, keepdims=True)
+        r.lsum[row_of(1, t)] = jnp.sum(s2, axis=0, keepdims=True)
         return carry
 
     lax.fori_loop(0, 13, tile, 0)
+
+    def keep_sums(lanes, whole):
+        q = whole[ROWS:]
+        r.og[0:1, lanes] = q[0:1] + q[1:2] + q[2:3]
+        r.og[1:2, lanes] = q[3:4] + q[4:5] + q[5:6]
 
     def unpermute(lo, hi, src):
         def step(g, carry):
             pair = jnp.concatenate([src(g), src(GROUPS)], axis=1)
-            p = dot(pair, r.pg[g], ((1,), (1,)))
-            r.xn[:, :, lanes_of(g)] = (acc[...] + p[:, :128]).astype(BF).reshape(14, 32, 128)
+            rows = jnp.concatenate([r.pn[:, lanes_of(g)], r.pn[:, 1536:1664]], axis=1)
+            p = dot(jnp.concatenate([pair, rows], axis=0), r.pg[g], ((1,), (1,)))
+            whole = acc[...] + p[:, :128]
             acc[...] = p[:, 128:]
+            r.xn[:, :, lanes_of(g)] = whole[0:ROWS].astype(BF).reshape(14, 32, 128)
+            keep_sums(lanes_of(g), whole)
             return carry
 
         if lo == 0:
@@ -553,7 +611,8 @@
         lax.fori_loop(lo, hi, step, 0)
 
     def write_out(raw, hbm, n):
-        r.xn[:, :, 1536:1664] = acc[...].astype(BF).reshape(14, 32, 128)
+        r.xn[:, :, 1536:1664] = acc[0:ROWS, :].astype(BF).reshape(14, 32, 128)
+        keep_sums(lanes_of(12), acc[...])
         for yy in range(14):
             raw[yy] = r.xn[yy, 0:28, 0:1584].reshape(14, 2, 1584)
         copy = pltpu.make_async_copy(raw, hbm, r.s_out.at[n])
@@ -563,19 +622,17 @@
     outs = []
     from_bo = lambda g: r.bo[:, lanes_of(g)]
     all_sum(1, r.lsum, r.gsum, [
-        lambda: unpermute(0, 4, from_bo),
-        lambda: unpermute(4, 8, from_bo),
-        lambda: unpermute(8, 12, from_bo),
-        lambda: outs.append(write_out(r.raw, r.out_hbm, 0)),
+        lambda: unpermute(0, 8, from_bo),
+        lambda: (unpermute(8, 12, from_bo), outs.append(write_out(r.raw, r.out_hbm, 0))),
     ])
 
     def gtile(t, carry):
         lanes = lanes_of(t)
-        avg = r.sums[0:1, lanes] / TOTAL
-        inv = lax.rsqrt(r.sums[1:2, lanes] / TOTAL - avg * avg + EPSILON)
-        scale = r.par[0:1, lanes] * inv
-        c1 = r.gsum[1:2, lanes] / TOTAL
-        c2 = r.gsum[0:1, lanes] / TOTAL
+        avg = r.sums[row_of(0, t)] / TOTAL
+        inv = lax.rsqrt(r.sums[row_of(1, t)] / TOTAL - avg * avg + EPSILON)
+        scale = r.par[row_of(0, t)] * inv
+        c1 = r.gsum[row_of(1, t)] / TOTAL
+        c2 = r.gsum[row_of(0, t)] / TOTAL
         normed = (r.hid[:, lanes].astype(F32) - avg) * inv
         gh = scale * (r.ga[:, lanes] - c1 - normed * c2)
         store_shifts(r.ghb, jnp.where(valid, gh, 0.0), lanes)
@@ -588,30 +645,44 @@
 
     st, r0 = r.st, r.r0
 
-    def place_of(k, i, half):
-        yy, xx = (y + 1 + k) % 4, (x + 1 + i) % 4
+    turns = (2, 1, 3, 0)
+    low, high = pl.ds(0, 256), pl.ds(256, 256)
+
+    def place_of(ay, ax, half):
+        yy, xx = (y + ay) % 4, (x + ax) % 4
         return yy * (1 - half) + xx * half, xx * (1 - half) + yy * half
 
-    def core_copy(k, i):
-        pv, pu = place_of(k, i, 1 - c)
+    def core_copy(ay, ax):
+        pv, pu = place_of(ay, ax, 1 - c)
         return pltpu.make_async_remote_copy(
             src_ref=st.at[1 - c, pv, pu], dst_ref=r0.at[pv, pu],
-            send_sem=r.s_c.at[4 * k + i], recv_sem=r.r_c.at[4 * k + i],
+            send_sem=r.s_c.at[4 * ay + ax], recv_sem=r.r_c.at[4 * ay + ax],
             device_id=sib, device_id_type=MESH,
         )
 
-    def v_copy(rel, ju):
-        q = (v + 1 + rel) % 4
+    def ring(m, ru):
+        rv, rows, dst, way = (
+            (2, low, r.ra.at[ru], 1),
+            (2, high, r.rb.at[ru], 3),
+            (1, high, r.rp.at[ru, high], 1),
+            (1, low, r.rp.at[ru, low], 1),
+            (3, low, r.rm.at[ru, low], 3),
+            (3, high, r.rm.at[ru, high], 3),
+        )[m]
         return pltpu.make_async_remote_copy(
-            src_ref=r0.at[q, (u + 1 + ju) % 4], dst_ref=r.r1.at[rel, ju],
-            send_sem=r.s_1.at[4 * rel + ju], recv_sem=r.r_1.at[4 * rel + ju],
-            device_id=at_v(q), device_id_type=MESH,
+            src_ref=r0.at[(v + rv) % 4, (u + ru) % 4, rows], dst_ref=dst,
+            send_sem=r.s_1.at[m, ru], recv_sem=r.r_1.at[m, ru],
+            device_id=at_v((v + way) % 4), device_id_type=MESH,
         )
 
-    def add_core(k):
-        for i in range(4):
-            core_copy(k, i).wait_recv()
-            pv, pu = place_of(k, i, c)
+    def launch(rv, ru):
+        for m in {2: (0, 1), 1: (2,), 3: (4,), 0: ()}[rv]:
+            ring(m, ru).start()
+
+    def add_core(ay):
+        for ax in turns:
+            core_copy(ay, ax).wait_recv()
+            pv, pu = place_of(ay, ax, c)
 
             def add(n, carry):
                 row = pl.ds(pl.multiple_of(n * 128, 128), 128)
@@ -620,17 +691,33 @@
                 return carry
 
             lax.fori_loop(0, 4, add, 0)
-            if i < 3:
+            if ax == ay:
+                launch(ay, ax)
+            else:
+                @pl.when(c == 0)
+                def _():
+                    launch(ay, ax)
+
                 @pl.when(c == 1)
                 def _():
-                    v_copy(i, k).start()
-
-            @pl.when((c == 0) & (k < 3))
-            def _():
-                v_copy(k, i).start()
-
-    def wstep(k, carry):
-        yy = (y + 1 + k) % 4
+                    launch(ax, ay)
+
+    def add_half(ru, m, buf, rv, start):
+        ring(m, ru).wait_recv()
+        pv, pu = (v + rv) % 4, (u + ru) % 4
+        for n in range(2):
+            row, own = pl.ds(128 * n, 128), pl.ds(start + 128 * n, 128)
+            total = r0[pv, pu, own, :].astype(F32) + buf[ru, row, :].astype(F32)
+            r0[pv, pu, own, :] = total.astype(BF)
+
+    def relay(ru):
+        add_half(ru, 0, r.ra, 1, 0)
+        ring(3, ru).start()
+        add_half(ru, 1, r.rb, 3, 256)
+        ring(5, ru).start()
+
+    def wstep(k):
+        yy = (y + turns[k]) % 4
         acc[0:144, :] = jnp.zeros((144, 128), F32)
         r.mec[...] = jnp.zeros_like(r.mec)
         lhs12 = r.g12t[rows_at(16 * yy, 16), :]
@@ -662,18 +749,16 @@
             st[1, px, yy, 496:512, :] = zeros[0:16]
         st[0, yy, 3, 384:512, :] = zeros
         st[1, 3, yy, 384:512, :] = zeros
-        for i in range(4):
-            core_copy(k, i).start()
-
-        @pl.when(k > 0)
-        def _():
-            add_core(k - 1)
-
-        return carry
-
-    lax.fori_loop(0, 4, wstep, 0)
-
-    def back_set(yy):
+        for ax in turns:
+            core_copy(turns[k], ax).start()
+        if k > 0:
+            add_core(turns[k - 1])
+
+    for k in range(4):
+        wstep(k)
+    add_core(turns[3])
+
+    def back_part(yy, lo, hi):
         block = pl.ds(128 + 16 * yy, 16)
         wt = r.wt
 
@@ -699,45 +784,53 @@
             r.gs[:, 1536:1664] += p[:, 128:]
             return carry
 
-        lax.fori_loop(0, 3, bstep, 0)
-        wt[block, :] = jnp.zeros((16, 1280), BF)
-
-    def sum_v(ju):
-        for rel in range(3):
-            v_copy(rel, ju).wait_recv()
-        pu = (u + 1 + ju) % 4
-
-        def add(n, carry):
-            row = pl.ds(pl.multiple_of(n * 128, 128), 128)
-            total = r0[v, pu, row, :].astype(F32)
-            for rel in range(3):
-                total = total + r.r1[rel, ju, row, :].astype(F32)
-            r.cur2[ju, row, :] = total.astype(BF)
-            return carry
-
-        lax.fori_loop(0, 4, add, 0)
-        if ju < 3:
-            send_u = send(r.cur2.at[ju], r.r2.at[ju], r.s_2.at[ju], r.r_2.at[ju], at_u(pu))
-            u_copies.append(send_u)
+        lax.fori_loop(lo, hi, bstep, 0)
+        if hi == 3:
+            wt[block, :] = jnp.zeros((16, 1280), BF)
 
     u_copies = []
-    back_set(0)
-    add_core(3)
-    back_set(1)
-    back_set(2)
-    sum_v(0)
-    sum_v(1)
-    back_set(3)
-    sum_v(2)
-    sum_v(3)
+
+    def sum_v(ru):
+        for m in range(2, 6):
+            ring(m, ru).wait_recv()
+        pu = (u + ru) % 4
+        for n in range(4):
+            row = pl.ds(128 * n, 128)
+            total = r0[v, pu, row, :].astype(F32) + r.rp[ru, row, :].astype(F32)
+            r.cur2[ru, row, :] = (total + r.rm[ru, row, :].astype(F32)).astype(BF)
+        if ru:
+            u_copies.append(
+                send(r.cur2.at[ru], r.r2.at[ru - 1], r.s_2.at[ru - 1], r.r_2.at[ru - 1], at_u(pu))
+            )
+
+    parts = [(yy, lo, hi) for yy in range(4) for lo, hi in ((0, 1), (1, 2), (2, 3))]
+
+    def back_next(n=1):
+        for _ in range(n):
+            if parts:
+                back_part(*parts.pop(0))
+
+    for ru in turns:
+        back_next()
+        relay(ru)
+    back_next()
+    for ru in turns:
+        back_next()
+        sum_v(ru)
+    back_next(12)
     from_gs = lambda g: r.gs[:, lanes_of(g)].astype(BF)
+    for t in range(13):
+        for n in range(2):
+            for k, part in enumerate(split3(r.gsum[n, t : t + 1, :])):
+                r.pf[3 * n + k : 3 * n + k + 1, lanes_of(t)] = part
+    r.pn[...] = r.pf[...].astype(BF)
     unpermute(0, 4, from_gs)
     for copy in u_copies:
         copy.wait_recv()
     sends += u_copies
     for n in range(8):
         row = pl.ds(64 * n, 64)
-        total = r.cur2[3, row, :].astype(F32)
+        total = r.cur2[0, row, :].astype(F32)
         for rel in range(3):
             total = total + r.r2[rel, row, :].astype(F32)
         r.cur3[n] = total.astype(BF)
@@ -762,6 +855,8 @@
     sends += copies
     unpermute(8, 12, from_gs)
     outs.append(write_out(r.raw2, r.ig_hbm, 1))
+    r.gg_out[...] = r.og[0:1, 0:1584].reshape(1584)
+    r.bg_out[...] = r.og[1:2, 0:1584].reshape(1584)
     for copy in copies:
         copy.wait_recv()
     near = [(1, 6 - 3 * (x % 2) - 3 * (x // 3)), (3, 3 - 3 * (x % 2))]
@@ -799,29 +894,31 @@
 
     for copy in sends:
         copy.wait_send()
-    for k in range(4):
-        for i in range(4):
-            core_copy(k, i).wait_send()
-    for rel in range(3):
-        for ju in range(4):
-            v_copy(rel, ju).wait_send()
+    for ay in range(4):
+        for ax in range(4):
+            core_copy(ay, ax).wait_send()
+    for m in range(6):
+        for ru in range(4):
+            ring(m, ru).wait_send()
     for copy in outs:
         copy.wait()
 
 
-def mega(idx, tiles, par, xt, upt):
+def mega(idx, tiles, gain, bias, xt, upt):
     k = constants()
-    operands = [idx, tiles, *prep_constants(), par, k["pg"], k["ry"], k["selm"], k["sele"], k["selb"], *fin_constants(), xt, upt]
+    operands = [idx, tiles, *prep_constants(), gain, bias]
+    operands += [k["pg"], k["ry"], k["selm"], k["sele"], k["selb"], *fin_constants(), xt, upt]
     anywhere = pl.BlockSpec(memory_space=pl.ANY)
     return pl.pallas_call(
         mega_body,
-        in_specs=[pl.BlockSpec(memory_space=pltpu.SMEM)] + [vspec()] * 15 + [anywhere] * 2,
-        out_specs=[anywhere, anywhere, vspec(), vspec()],
+        in_specs=[pl.BlockSpec(memory_space=pltpu.SMEM)] + [vspec()] * 9 + [anywhere] * 9,
+        out_specs=[anywhere, anywhere, vspec(), vspec(), vspec()],
         out_shape=[
             struct((14, 14, 2, 1584), BF),
             struct((14, 14, 2, 1584), BF),
             struct((396, GW), F32),
-            struct((2, LANES), F32),
+            struct((1584,), F32),
+            struct((1584,), F32),
         ],
         scratch_shapes=list(scratch_list().values()),
         compiler_params=pltpu.CompilerParams(
@@ -831,44 +928,59 @@
     )(*operands)
 
 
-def channels_in(v):
-    p = v.reshape(4, 3, 4, 33)
-    main = p[..., :32].reshape(1536)
-    extra = jnp.pad(p[..., 32].reshape(4, 12), ((0, 0), (0, 4))).reshape(64)
-    return jnp.concatenate([main, extra, jnp.zeros((64,), v.dtype)])
-
-
-def channels_out(v):
-    main = v[:1536].reshape(4, 3, 4, 32)
-    extra = v[1536:1600].reshape(4, 16)[:, :12].reshape(4, 3, 4, 1)
-    return jnp.concatenate([main, extra], axis=-1).reshape(1584)
+def finish_body(out_a, ig_a, out_b, ig_b, one, two, sem):
+    pairs = [(out_a, one, out_b), (ig_a, two, ig_b)]
+    loads = [pltpu.make_async_copy(src, mid, sem.at[n]) for n, (src, mid, _) in enumerate(pairs)]
+    saves = [pltpu.make_async_copy(mid, dst, sem.at[2 + n]) for n, (_, mid, dst) in enumerate(pairs)]
+    for load in loads:
+        load.start()
+    for load, save in zip(loads, saves):
+        load.wait()
+        save.start()
+    for save in saves:
+        save.wait()
+
+
+def finish(out, ig):
+    anywhere = pl.BlockSpec(memory_space=pl.ANY)
+    return pl.pallas_call(
+        finish_body,
+        in_specs=[anywhere] * 2,
+        out_specs=[anywhere] * 2,
+        out_shape=[struct((14, 14, 2, 1584), BF)] * 2,
+        scratch_shapes=[VM((14, 14, 2, 1584), BF)] * 2 + [DMA((4,))],
+        name="finish",
+    )(out, ig)
 
 
 def tile_rows(tile_counts, owner_order):
-    run_end = jnp.cumsum(tile_counts)
+    ranks = jnp.arange(64, dtype=jnp.int32)
+    upto = (ranks[None, :] <= ranks[:, None]).astype(jnp.int32)
+    run_end = jnp.sum(upto * tile_counts[None, :], axis=1)
     run_start = run_end - tile_counts
-    tile_ids = jnp.arange(144, dtype=jnp.int32)
-    rank_of = jnp.sum((run_end[None, :] <= tile_ids[:, None]).astype(jnp.int32), axis=1)
-    onehot = (rank_of[:, None] == jnp.arange(64, dtype=jnp.int32)[None, :]).astype(jnp.int32)
-    s = jnp.sum(onehot * owner_order[None, :], axis=1)
-    j = tile_ids - jnp.sum(onehot * run_start[None, :], axis=1)
+    t = jnp.arange(144, dtype=jnp.int32)[:, None]
+    j = t - run_start[None, :]
+    s = owner_order[None, :]
     y, zl, x, core = s // 16, (s // 8) % 2, (s // 2) % 4, s % 2
     vu = jnp.where(j < 2, y * 4 + x, x * 4 + y)
-    return (j // 2) * 128 + vu * 8 + zl * 4 + core * 2 + j % 2
+    spot = (j // 2) * 128 + vu * 8 + zl * 4 + core * 2 + j % 2
+    held = (j >= 0) & (t < run_end[None, :])
+    return jnp.sum(jnp.where(held, spot, 0), axis=1)
 
 
 def local(block_input, upstream, kernel_tiles, tile_counts, owner_order, gain, bias):
     idx = tile_rows(tile_counts, owner_order)
-    par = jnp.stack([channels_in(gain), channels_in(bias)])
     turn = lambda a: jnp.transpose(a, (1, 2, 0, 3))
     back = lambda a: jnp.transpose(a, (2, 0, 1, 3))
-    out, ig, kg, gsum = mega(
-        idx, kernel_tiles.reshape(4, 99, GW), par, turn(block_input), turn(upstream)
+    out, ig, kg, gg, bg = mega(
+        idx, kernel_tiles.reshape(4, 99, GW), gain, bias,
+        turn(block_input), turn(upstream),
     )
+    out, ig = finish(out, ig)
     sp = lax.axis_index("shard") % 16
     b0 = (sp * 29403) // 17424 - sp // 15
     kernel_grad = lax.dynamic_slice(kg.reshape(-1), (sp * 29403 - b0 * 17424,), (29403,))
-    return (back(out), back(ig), kernel_grad, channels_out(gsum[0]), channels_out(gsum[1]))
+    return (back(out), back(ig), kernel_grad, gg, bg)
 
 
 def solution(mesh):

time: 138 us -> 125 us (0.906)
  local copies, waits for them, and re-layouts: 15.3 us -> 5.13 us
  Pallas kernels: 118 us -> 116 us
    pallas_call x1, Pallas kernels: 118 us -> 113 us  [mega(): pl.pallas_call(mega_body, in_specs=[pl.BlockSpec(memory_space=pltpu.SMEM)...]
    reshape x14 -> x0, local copies, waits for them, and re-layouts: 3.97 us -> none  [the longest x2 1.65 us: channels_in(): p = v.reshape(4, 3, 4, 33)]
    unnamed x4 -> x6, local copies, waits for them, and re-layouts: 4.42 us -> 1.21 us
    pallas_call x0 -> x1, Pallas kernels: none -> 2.86 us  [finish(): pl.pallas_call(finish_body, in_specs=[anywhere] * 2, out_specs=[anywhere]...]
    slice x4 -> x0, local copies, waits for them, and re-layouts: 1.93 us -> none  [the longest x1 0.82 us: channels_out(): main = v[:1536].reshape(4, 3, 4, 32)]
where the time goes in v3:
time: 125 us
  Pallas kernels  116 us (93%)
  local copies, waits for them, and re-layouts  5.13 us (4%)
  other arithmetic  2.85 us (2%)
    pallas_call x1, Pallas kernels, mega(): pl.pallas_call(mega_body, in_specs=[pl.BlockSpec(memory_space=pltpu.SMEM)...  113 us
    pallas_call x1, Pallas kernels, finish(): pl.pallas_call(finish_body, in_specs=[anywhere] * 2, out_specs=[anywhere]...  2.86 us

profile of v3, /device:TPU:1, one launch (start us, length us, event | category | flops | bytes accessed | tf_op | source)
XLA Modules:
  0.0 124.6 jit_solution(6423251378968275869)
XLA Ops:
  0.7 0.7 multiply_add_fusion.1
  1.4 0.8 select_reduce_fusion
  2.2 0.7 sub.52
  2.8 0.7 fusion.11.refs_0_
  3.6 1.9 %reshape.99.refs_1_ = bf16[4,99,132]{2,1,0:T(8,128)(2,1)} reshape(bf16[4,13068]{1,0:T(4,128)(2,1)} %param.22) | data formatting | bytes 209088 | tf_op jit(solution)/shard_map/reshape | solution.py:976
  5.4 113.1 %block.1 = (bf16[14,14,2,1584]{3,2,1,0:T(2,128)(2,1)}, bf16[14,14,2,1584]{3,2,1,0:T(2,128)(2,1)}, f32[396,132]{1,0:T(8,128)}, f32[1584]{0:T(1024)}, f32[1584]{0:T(1024)}) custom-call(s32[144]{0:T(256)} %fusion.11.refs_0_, bf16[4,99,132]{2,1,0:T(8,128)(2,1)} %reshape.99.refs_1_, bf16[132,128]{1,0:T(8,128)(2,1)} %constant.151.clone.refs_2_, ...), custom_call_target="tpu_custom_call" | custom-call | tf_op jit(solution)/shard_map/block/pallas_call | solution.py:912
  118.5 1.3 %reshape.100 = f32[52272]{0:T(1024)S(1)} reshape(f32[396,132]{1,0:T(8,128)} %get-tuple-element.16) | data formatting | bytes 418176 | tf_op jit(solution)/shard_map/reshape | solution.py:982
  119.8 0.8 dynamic_slice.3
  120.5 0.0 copy-start.1
  120.6 0.0 copy-start
  120.6 2.9 %finish.1 = (bf16[14,14,2,1584]{3,2,1,0:T(2,128)(2,1)}, bf16[14,14,2,1584]{3,2,1,0:T(2,128)(2,1)}) custom-call(bf16[14,14,2,1584]{3,2,1,0:T(2,128)(2,1)} %get-tuple-element.12.out_a, bf16[14,14,2,1584]{3,2,1,0:T(2,128)(2,1)} %get-tuple-element.13.ig_a), custom_call_target="tpu_custom_call" | custom-call | tf_op jit(solution)/shard_map/finish/pallas_call | solution.py:946
  123.4 0.0 copy-done.1
  123.4 0.6 copy.27
  124.0 0.0 copy-done
  124.0 0.6 copy.28
  (1 shorter events, 0.0 us)
Async XLA Ops:
  120.5 2.9 %copy-start.1 = (f32[1584]{0:T(1024)S(1)}, f32[1584]{0:T(1024)}, u32[]{:S(2)}) copy-start(f32[1584]{0:T(1024)} %get-tuple-element.32) | copy-start | bytes 19012
  120.6 3.5 %copy-start = (f32[1584]{0:T(1024)S(1)}, f32[1584]{0:T(1024)}, u32[]{:S(2)}) copy-start(f32[1584]{0:T(1024)} %get-tuple-element.33) | copy-start | bytes 19012

commit v4 on v3

--- a/solution.py
+++ b/solution.py
@@ -213,7 +213,8 @@
         xn=VM((14, 32, LANES), BF),
         acc=VM((ROWS + 16, 128), F32),
         mec=VM((16, 1152), F32),
-        bg=VM((1280, 256), BF),
+        bg=VM((3, 1280, 256), BF),
+        kgs=VM((416, 256), F32),
         wt=VM((256, 1280), BF),
         tr=VM((128, 512), BF),
         g12t=VM((128, ROWS), BF),
@@ -256,10 +257,10 @@
         s_3=DMA((7,)), r_3=DMA((7,)),
         s_4=DMA((7,)), r_4=DMA((7,)),
         s_5=DMA((11,)), r_5=DMA((11,)),
-        s_a=DMA((2, 25)), r_a=DMA((2, 25)),
+        s_a=DMA((2, 33)), r_a=DMA((2, 33)),
         buf_c=VM((2, 16, 128), F32),
         buf_p=VM((2, 16, 16, 128), F32),
-        buf_z=VM((2, 8, 16, 128), F32),
+        buf_z=VM((2, 2, 8, 16, 128), F32),
     )
     return sets
 
@@ -289,7 +290,7 @@
     others = [sib]
     others += [device((x + k % 4) % 4, (y + k // 4) % 4, z, c) for k in range(1, 16)]
     others += [device((x + k) % 4, y, z, 1 - c) for k in range(1, 4)]
-    others += [device(x, y, (z + k) % 8, c) for k in range(1, 8)]
+    others += [device(x, y, (z + k) % 8, cc) for k in range(1, 8) for cc in (c, 1 - c)]
     barrier = pltpu.get_barrier_semaphore()
     for d in others:
         pl.semaphore_signal(barrier, inc=1, device_id=d, device_id_type=MESH)
@@ -504,7 +505,7 @@
         for gg in range(3):
             g = 3 * yy + gg
             here = (lane_iota(1152) // 4) == yy * 4 + gg
-            bg = r.bg
+            bg = r.bg.at[gg]
             bg[0:1152, 0:128] = r.bm[g]
             bg[0:1152, 128:256] = jnp.where(here, r.me[...].astype(F32), 0.0).astype(BF)
             tails = r.ta[g].reshape(192, 128)
@@ -525,32 +526,38 @@
     stat(h, 12)
 
     def all_sum(k, src, dst, fill):
-        def share(buf, n, p, base, dev):
+        def share(buf, p, base, partners):
             copies = [
-                send(buf.at[p], buf.at[p], r.s_a.at[k, base + i], r.r_a.at[k, base + i], dev((p + i) % n))
-                for i in range(1, n)
+                send(buf.at[p], buf.at[p], r.s_a.at[k, base + i], r.r_a.at[k, base + i], to)
+                for i, to in enumerate(partners)
             ]
             sends.extend(copies)
             if fill:
                 fill.pop(0)()
             for copy in copies:
                 copy.wait_recv()
-            total = buf[0]
+
+        def total(buf, n):
+            out = buf[0]
             for i in range(1, n):
-                total = total + buf[i]
-            return total
+                out = out + buf[i]
+            return out
 
         half = send(src.at[1 - c], r.buf_c.at[k], r.s_a.at[k, 0], r.r_a.at[k, 0], sib)
         half.wait_recv()
         plane, line = r.buf_p.at[k], r.buf_z.at[k]
         p = y * 4 + x
         plane[p] = src[c] + r.buf_c[k]
-        line[z] = share(plane, 16, p, 0, lambda q: device(q % 4, q // 4, z, c))
-        dst[c] = share(line, 8, z, 16, lambda q: device(x, y, q, c))
-        rest = send(dst.at[c], dst.at[c], r.s_a.at[k, 24], r.r_a.at[k, 24], sib)
-        rest.wait_recv()
+        over = [(p + i) % 16 for i in range(1, 16)]
+        share(plane, p, 1, [device(q % 4, q // 4, z, c) for q in over])
+        mine = line.at[c]
+        mine[z] = total(plane, 16)
+        along = [device(x, y, (z + i) % 8, c) for i in range(1, 8)]
+        along += [device(x, y, (z + i) % 8, 1 - c) for i in range(8)]
+        share(mine, z, 16, along)
+        for n in range(2):
+            dst[n] = total(line.at[n], 8)
         half.wait_send()
-        sends.append(rest)
 
     def make_tr():
         tr_in = jnp.concatenate([r.me[128 * tap : 128 * tap + 128] for tap in range(9)], axis=1)
@@ -817,14 +824,13 @@
     for ru in turns:
         back_next()
         sum_v(ru)
-    back_next(12)
+    back_next()
     from_gs = lambda g: r.gs[:, lanes_of(g)].astype(BF)
     for t in range(13):
         for n in range(2):
             for k, part in enumerate(split3(r.gsum[n, t : t + 1, :])):
                 r.pf[3 * n + k : 3 * n + k + 1, lanes_of(t)] = part
     r.pn[...] = r.pf[...].astype(BF)
-    unpermute(0, 4, from_gs)
     for copy in u_copies:
         copy.wait_recv()
     sends += u_copies
@@ -839,7 +845,7 @@
         q = (z + k) % 8
         copies.append(send(r.cur3.at[q], r.r3.at[k - 1], r.s_3.at[k - 1], r.r_3.at[k - 1], device(x, y, q, c)))
     sends += copies
-    unpermute(4, 8, from_gs)
+    back_next(12)
     for copy in copies:
         copy.wait_recv()
     total = r.cur3[z].astype(F32)
@@ -853,10 +859,7 @@
         q = (z + k) % 8
         copies.append(send(here, here, r.s_4.at[k - 1], r.r_4.at[k - 1], device(x, y, q, c)))
     sends += copies
-    unpermute(8, 12, from_gs)
-    outs.append(write_out(r.raw2, r.ig_hbm, 1))
-    r.gg_out[...] = r.og[0:1, 0:1584].reshape(1584)
-    r.bg_out[...] = r.og[1:2, 0:1584].reshape(1584)
+    unpermute(0, 8, from_gs)
     for copy in copies:
         copy.wait_recv()
     near = [(1, 6 - 3 * (x % 2) - 3 * (x // 3)), (3, 3 - 3 * (x % 2))]
@@ -871,6 +874,10 @@
         to = device((x + 2) % 4, y, z, cc)
         copies.append(send(hh.at[c, x, 7], hh.at[c, x, 7], r.s_5.at[n], r.r_5.at[n], to))
         n += 1
+    unpermute(8, 12, from_gs)
+    outs.append(write_out(r.raw2, r.ig_hbm, 1))
+    r.gg_out[...] = r.og[0:1, 0:1584].reshape(1584)
+    r.bg_out[...] = r.og[1:2, 0:1584].reshape(1584)
     for copy in copies:
         copy.wait_recv()
     sends += copies
@@ -890,7 +897,19 @@
         qe = jnp.where((line >= 0) & (line < 4) & (unit == 33 * line + 32), 1.0, 0.0).astype(BF)
         t1 = (dot(left, r.qm[...]) + dot(em, qe)).astype(BF)
         t2 = dot(t1, r.qo[gg], ((0,), (0,)))
-        r.kg[pl.ds(132 * k, 132), :] = t2[0:132]
+        r.kgs[132 * k : 132 * k + 132, 0:GW] = t2[0:132]
+
+    lane = lane_iota(32)
+    skip = 4 * lax.broadcasted_iota(jnp.int32, (32, 128), 0)
+    for k in range(13):
+        rows = r.kgs[32 * k : 32 * k + 32, :]
+        body = pltpu.roll(rows[:, 0:128], 0, 1, stride=4, stride_axis=0)
+        rest = pltpu.roll(rows[:, 128:256], 0, 1, stride=4, stride_axis=0)
+        head = jnp.where(lane >= skip, body, 0.0)
+        tail = jnp.where(lane < skip, body, jnp.where(lane < skip + 4, rest, 0.0))
+        r.kg[33 * k : 33 * k + 32, :] = head
+        r.kg[33 * k + 32 : 33 * k + 33, :] = jnp.zeros((1, 128), F32)
+        r.kg[33 * k + 1 : 33 * k + 33, :] += tail
 
     for copy in sends:
         copy.wait_send()
@@ -916,7 +935,7 @@
         out_shape=[
             struct((14, 14, 2, 1584), BF),
             struct((14, 14, 2, 1584), BF),
-            struct((396, GW), F32),
+            struct((432, 128), F32),
             struct((1584,), F32),
             struct((1584,), F32),
         ],
@@ -955,16 +974,14 @@
 
 def tile_rows(tile_counts, owner_order):
     ranks = jnp.arange(64, dtype=jnp.int32)
-    upto = (ranks[None, :] <= ranks[:, None]).astype(jnp.int32)
-    run_end = jnp.sum(upto * tile_counts[None, :], axis=1)
-    run_start = run_end - tile_counts
-    t = jnp.arange(144, dtype=jnp.int32)[:, None]
-    j = t - run_start[None, :]
+    before = (ranks[None, :] < ranks[:, None]).astype(jnp.int32)
+    run_start = jnp.sum(before * tile_counts[None, :], axis=1)
+    j = jnp.arange(144, dtype=jnp.int32)[:, None] - run_start[None, :]
     s = owner_order[None, :]
     y, zl, x, core = s // 16, (s // 8) % 2, (s // 2) % 4, s % 2
     vu = jnp.where(j < 2, y * 4 + x, x * 4 + y)
     spot = (j // 2) * 128 + vu * 8 + zl * 4 + core * 2 + j % 2
-    held = (j >= 0) & (t < run_end[None, :])
+    held = (j >= 0) & (j < tile_counts[None, :])
     return jnp.sum(jnp.where(held, spot, 0), axis=1)
 
 

time: 125 us -> 124 us (level)
    reshape x1 -> x0, local copies, waits for them, and re-layouts: 1.28 us -> none  [local(): kg.reshape(-1)]
where the time goes in v4:
time: 124 us
  Pallas kernels  116 us (94%)
  local copies, waits for them, and re-layouts  4.76 us (4%)
  other arithmetic  2.84 us (2%)
    pallas_call x1, Pallas kernels, mega(): pl.pallas_call(mega_body, in_specs=[pl.BlockSpec(memory_space=pltpu.SMEM)...  113 us
    pallas_call x1, Pallas kernels, finish(): pl.pallas_call(finish_body, in_specs=[anywhere] * 2, out_specs=[anywhere]...  2.86 us

profile of v4, /device:TPU:1, one launch (start us, length us, event | category | flops | bytes accessed | tf_op | source)
XLA Modules:
  0.0 123.8 jit_solution(9980974693712072954)
XLA Ops:
  0.7 0.7 multiply_add_fusion.1
  1.4 0.8 select_reduce_fusion
  2.2 1.4 %fusion.12.refs_0_ = s32[144]{0:T(256)} fusion(s32[64]{0:T(128)S(1)} %get-tuple-element.22, s32[64]{0:T(128)S(1)} %get-tuple-element.23, s32[64]{0:T(128)S(1)} %multiply_add_fusion, s32[64]{0:T(128)S(1)} %get-tuple-element.19, s32[64]{0:T(128)} %param.23, s32[64]{0:T(128)S(1)} %select_reduce_fusion), kind=kLoop, calls=%fused_computation.19 | loop fusion | flops 303984 | bytes 2112 | tf_op jit(solution)/shard_map/reduce_sum | solution.py:985
  3.6 1.9 %reshape.98.refs_1_ = bf16[4,99,132]{2,1,0:T(8,128)(2,1)} reshape(bf16[4,13068]{1,0:T(4,128)(2,1)} %param.22) | data formatting | bytes 209088 | tf_op jit(solution)/shard_map/reshape | solution.py:993
  5.4 112.6 %block.1 = (bf16[14,14,2,1584]{3,2,1,0:T(2,128)(2,1)}, bf16[14,14,2,1584]{3,2,1,0:T(2,128)(2,1)}, f32[432,128]{1,0:T(8,128)}, f32[1584]{0:T(1024)}, f32[1584]{0:T(1024)}) custom-call(s32[144]{0:T(256)} %fusion.12.refs_0_, bf16[4,99,132]{2,1,0:T(8,128)(2,1)} %reshape.98.refs_1_, bf16[132,128]{1,0:T(8,128)(2,1)} %constant.151.clone.refs_2_, ...), custom_call_target="tpu_custom_call" | custom-call | tf_op jit(solution)/shard_map/block/pallas_call | solution.py:931
  118.1 1.7 %dynamic_slice.3 = f32[29403]{0:T(1024)} dynamic-slice(f32[55296]{0:T(1024)} %bitcast.7, s32[]{:T(128)S(6)} %select_n.80), dynamic_slice_sizes={29403} | dynamic-slice | bytes 235228 | tf_op jit(solution)/shard_map/dynamic_slice | solution.py:999
  119.8 0.0 copy-start.1
  119.8 0.0 copy-start
  119.8 2.9 %finish.1 = (bf16[14,14,2,1584]{3,2,1,0:T(2,128)(2,1)}, bf16[14,14,2,1584]{3,2,1,0:T(2,128)(2,1)}) custom-call(bf16[14,14,2,1584]{3,2,1,0:T(2,128)(2,1)} %get-tuple-element.12.out_a, bf16[14,14,2,1584]{3,2,1,0:T(2,128)(2,1)} %get-tuple-element.13.ig_a), custom_call_target="tpu_custom_call" | custom-call | tf_op jit(solution)/shard_map/finish/pallas_call | solution.py:965
  122.6 0.0 copy-done.1
  122.6 0.6 copy.27
  123.2 0.0 copy-done
  123.2 0.6 copy.28
  (1 shorter events, 0.0 us)
Async XLA Ops:
  119.8 2.9 %copy-start.1 = (f32[1584]{0:T(1024)S(1)}, f32[1584]{0:T(1024)}, u32[]{:S(2)}) copy-start(f32[1584]{0:T(1024)} %get-tuple-element.32) | copy-start | bytes 19012
  119.8 3.5 %copy-start = (f32[1584]{0:T(1024)S(1)}, f32[1584]{0:T(1024)}, u32[]{:S(2)}) copy-start(f32[1584]{0:T(1024)} %get-tuple-element.33) | copy-start | bytes 19012

commit v5 on v4

--- a/solution.py
+++ b/solution.py
@@ -947,10 +947,10 @@
     )(*operands)
 
 
-def finish_body(out_a, ig_a, out_b, ig_b, one, two, sem):
-    pairs = [(out_a, one, out_b), (ig_a, two, ig_b)]
-    loads = [pltpu.make_async_copy(src, mid, sem.at[n]) for n, (src, mid, _) in enumerate(pairs)]
-    saves = [pltpu.make_async_copy(mid, dst, sem.at[2 + n]) for n, (_, mid, dst) in enumerate(pairs)]
+def finish_body(*refs):
+    srcs, dsts, mids, sem = refs[0:4], refs[4:8], refs[8:12], refs[12]
+    loads = [pltpu.make_async_copy(a, b, sem.at[0, n]) for n, (a, b) in enumerate(zip(srcs, mids))]
+    saves = [pltpu.make_async_copy(a, b, sem.at[1, n]) for n, (a, b) in enumerate(zip(mids, dsts))]
     for load in loads:
         load.start()
     for load, save in zip(loads, saves):
@@ -960,16 +960,16 @@
         save.wait()
 
 
-def finish(out, ig):
+def finish(*arrays):
     anywhere = pl.BlockSpec(memory_space=pl.ANY)
     return pl.pallas_call(
         finish_body,
-        in_specs=[anywhere] * 2,
-        out_specs=[anywhere] * 2,
-        out_shape=[struct((14, 14, 2, 1584), BF)] * 2,
-        scratch_shapes=[VM((14, 14, 2, 1584), BF)] * 2 + [DMA((4,))],
+        in_specs=[anywhere] * 4,
+        out_specs=[anywhere] * 4,
+        out_shape=[struct(a.shape, a.dtype) for a in arrays],
+        scratch_shapes=[VM(a.shape, a.dtype) for a in arrays] + [DMA((2, 4))],
         name="finish",
-    )(out, ig)
+    )(*arrays)
 
 
 def tile_rows(tile_counts, owner_order):
@@ -993,7 +993,7 @@
         idx, kernel_tiles.reshape(4, 99, GW), gain, bias,
         turn(block_input), turn(upstream),
     )
-    out, ig = finish(out, ig)
+    out, ig, gg, bg = finish(out, ig, gg, bg)
     sp = lax.axis_index("shard") % 16
     b0 = (sp * 29403) // 17424 - sp // 15
     kernel_grad = lax.dynamic_slice(kg.reshape(-1), (sp * 29403 - b0 * 17424,), (29403,))

time: 124 us -> 122 us (0.984)
  local copies, waits for them, and re-layouts: 4.76 us -> 2.65 us
where the time goes in v5:
time: 122 us
  Pallas kernels  116 us (95%)
  other arithmetic  2.84 us (2%)
  local copies, waits for them, and re-layouts  2.65 us (2%)
    pallas_call x1, Pallas kernels, mega(): pl.pallas_call(mega_body, in_specs=[pl.BlockSpec(memory_space=pltpu.SMEM)...  113 us
    pallas_call x1, Pallas kernels, finish(): pl.pallas_call(finish_body, in_specs=[anywhere] * 4, out_specs=[anywhere]...  2.91 us

profile of v5, /device:TPU:1, one launch (start us, length us, event | category | flops | bytes accessed | tf_op | source)
XLA Modules:
  0.0 121.8 jit_solution(11050877525459020004)
XLA Ops:
  0.6 0.7 multiply_add_fusion.1
  1.3 0.8 select_reduce_fusion
  2.1 1.4 %fusion.12.refs_0_ = s32[144]{0:T(256)} fusion(s32[64]{0:T(128)S(1)} %get-tuple-element.26, s32[64]{0:T(128)S(1)} %get-tuple-element.27, s32[64]{0:T(128)S(1)} %multiply_add_fusion, s32[64]{0:T(128)S(1)} %get-tuple-element.23, s32[64]{0:T(128)} %param.23, s32[64]{0:T(128)S(1)} %select_reduce_fusion), kind=kLoop, calls=%fused_computation.19 | loop fusion | flops 303984 | bytes 2112 | tf_op jit(solution)/shard_map/reduce_sum | solution.py:985
  3.5 1.9 %reshape.98.refs_1_ = bf16[4,99,132]{2,1,0:T(8,128)(2,1)} reshape(bf16[4,13068]{1,0:T(4,128)(2,1)} %param.22) | data formatting | bytes 209088 | tf_op jit(solution)/shard_map/reshape | solution.py:993
  5.4 112.6 %block.1 = (bf16[14,14,2,1584]{3,2,1,0:T(2,128)(2,1)}, bf16[14,14,2,1584]{3,2,1,0:T(2,128)(2,1)}, f32[432,128]{1,0:T(8,128)}, f32[1584]{0:T(1024)}, f32[1584]{0:T(1024)}) custom-call(s32[144]{0:T(256)} %fusion.12.refs_0_, bf16[4,99,132]{2,1,0:T(8,128)(2,1)} %reshape.98.refs_1_, bf16[132,128]{1,0:T(8,128)(2,1)} %constant.151.clone.refs_2_, ...), custom_call_target="tpu_custom_call" | custom-call | tf_op jit(solution)/shard_map/block/pallas_call | solution.py:931
  118.0 0.0 copy-start
  118.0 2.9 %finish.1 = (bf16[14,14,2,1584]{3,2,1,0:T(2,128)(2,1)}, bf16[14,14,2,1584]{3,2,1,0:T(2,128)(2,1)}, f32[1584]{0:T(1024)}, f32[1584]{0:T(1024)}) custom-call(bf16[14,14,2,1584]{3,2,1,0:T(2,128)(2,1)} %get-tuple-element.14.refs_0_, bf16[14,14,2,1584]{3,2,1,0:T(2,128)(2,1)} %get-tuple-element.15.refs_1_, f32[1584]{0:T(1024)} %get-tuple-element.16.refs_2_, ...), custom_call_target="tpu_custom_call" | custom-call | tf_op jit(solution)/shard_map/finish/pallas_call | solution.py:965
  121.0 0.0 copy-done
  121.0 0.8 dynamic_slice.3
  (1 shorter events, 0.0 us)
Async XLA Ops:
  118.0 3.0 %copy-start = (f32[432,128]{1,0:T(8,128)S(1)}, f32[432,128]{1,0:T(8,128)}, u32[]{:S(2)}) copy-start(f32[432,128]{1,0:T(8,128)} %get-tuple-element.20) | copy-start | bytes 663556
